TPU v7x, 256 devices: a whole 4x4x8 slice. The times are simulated.
256 devices in a mesh: ctx: 4 (over z_lo), resp: 32 (over x, y, core), head: 2 (over z_hi).
Axes of the slice: x: 4, y: 4, z: 8 (z_hi: 2, z_lo: 4; z = z_hi * 4 + z_lo), core: 2. Of those that a mesh axis runs over, the one named last changes fastest.
Arguments:
- queries: bfloat16 [32, 768, 32, 128], P('resp', 'ctx', 'head'), may hold values from -110 to 110
- grad_out: bfloat16 [32, 768, 32, 128], P('resp', 'ctx', 'head'), may hold values from -6 to 6
- resp_keys: bfloat16 [32, 768, 8, 128], P('resp', 'ctx', 'head'), may hold values from -6 to 6
- resp_values: bfloat16 [32, 768, 8, 128], P('resp', 'ctx', 'head'), may hold values from -6 to 6
- prompt_keys: bfloat16 [1536, 8, 128], P('ctx', 'head'), may hold values from -4 to 4
- prompt_values: bfloat16 [1536, 8, 128], P('ctx', 'head'), may hold values from -6 to 6
- resp_lengths: int32 [32], P('resp'), may hold values from 1 to 768, 18432 in all
Outputs:
- d_queries: bfloat16 [32, 768, 32, 128], P('resp', 'ctx', 'head')
- d_resp_keys: bfloat16 [32, 768, 8, 128], P('resp', 'ctx', 'head')
- d_resp_values: bfloat16 [32, 768, 8, 128], P('resp', 'ctx', 'head')
- d_prompt_keys: bfloat16 [1536, 8, 128], P(('ctx', 'resp'), 'head')
- d_prompt_values: bfloat16 [1536, 8, 128], P(('ctx', 'resp'), 'head')
Inputs may be any that keep to these rules, and one draw needn't show every extreme that they name: `resp_lengths`: the longest response has exactly 768 positions.
All inputs are finite; a program needn't handle non-finite values. No bound on the sum of `resp_lengths` on one device may be relied on, other than what follows from the above.
Results may differ from a plain program's by a relative error of at most 0.02.
Values may be sent and summed in bfloat16 or wider, within the bound.
A program may use at most 192 MiB of HBM per device.

v0:
```python
import jax
import jax.numpy as jnp
from jax import lax
from jax.sharding import PartitionSpec as P


def local_group(query_group, grad_group, key_group, value_group, first_row, length, prompt_count):
    scale = query_group.shape[-1] ** (-0.5)
    row_count = query_group.shape[0]
    key_count = key_group.shape[0]
    scores = (
        jnp.einsum("tqd,jd->qtj", query_group, key_group, preferred_element_type=jnp.float32)
        * scale
    )
    position = first_row + jnp.arange(row_count, dtype=jnp.int32)[:, None]
    key_index = jnp.arange(key_count, dtype=jnp.int32)[None, :]
    resp_index = key_index - prompt_count
    allowed = (key_index < prompt_count) | (resp_index <= position) & (resp_index < length)
    scores = jnp.where(allowed[None], scores, -jnp.inf)
    row_max = jnp.max(scores, axis=-1, keepdims=True)
    exponent = jnp.exp(scores - row_max)
    weights = exponent / jnp.sum(exponent, axis=-1, keepdims=True)
    weights_low = weights.astype(jnp.bfloat16)
    grad_weights = jnp.einsum(
        "tqd,jd->qtj", grad_group, value_group, preferred_element_type=jnp.float32
    )
    row_delta = jnp.sum(weights * grad_weights, axis=-1, keepdims=True)
    grad_scores = (weights * (grad_weights - row_delta) * scale).astype(jnp.bfloat16)
    grad_query = jnp.einsum(
        "qtj,jd->tqd", grad_scores, key_group, preferred_element_type=jnp.float32
    )
    grad_key = jnp.einsum(
        "qtj,tqd->jd", grad_scores, query_group, preferred_element_type=jnp.float32
    )
    grad_value = jnp.einsum(
        "qtj,tqd->jd", weights_low, grad_group, preferred_element_type=jnp.float32
    )
    return (grad_query, grad_key, grad_value)


def on_device(queries, grad_out, resp_keys, resp_values, prompt_keys, prompt_values, resp_lengths):
    row_count = queries.shape[1]
    head_count = queries.shape[2]
    kv_count = prompt_keys.shape[1]
    group_size = head_count // kv_count
    full_prompt_keys, full_prompt_values = (
        lax.all_gather(prompt_keys, "ctx", axis=0, tiled=True),
        lax.all_gather(prompt_values, "ctx", axis=0, tiled=True),
    )
    full_resp_keys, full_resp_values = (
        lax.all_gather(resp_keys, "ctx", axis=1, tiled=True),
        lax.all_gather(resp_values, "ctx", axis=1, tiled=True),
    )
    prompt_count = full_prompt_keys.shape[0]
    all_keys = jnp.concatenate([full_prompt_keys, full_resp_keys[0]], 0)
    all_values = jnp.concatenate([full_prompt_values, full_resp_values[0]], 0)
    first_row = lax.axis_index("ctx") * row_count
    length = resp_lengths[0]
    position = first_row + jnp.arange(row_count, dtype=jnp.int32)
    grad_rows = jnp.where(
        (position < length)[:, None, None], grad_out[0], jnp.zeros_like(grad_out[0])
    )
    query_rows = queries[0]
    query_parts = []
    key_parts = []
    value_parts = []
    for group_index in range(kv_count):
        lower = group_index * group_size
        upper = lower + group_size
        grad_query, grad_key, grad_value = local_group(
            query_rows[:, lower:upper],
            grad_rows[:, lower:upper],
            all_keys[:, group_index],
            all_values[:, group_index],
            first_row,
            length,
            prompt_count,
        )
        query_parts.append(grad_query)
        key_parts.append(grad_key)
        value_parts.append(grad_value)
    grad_queries = jnp.concatenate(query_parts, 1).astype(jnp.bfloat16)[None]
    key_total = jnp.stack(key_parts, 1)
    value_total = jnp.stack(value_parts, 1)
    prompt_key_part = key_total[:prompt_count]
    prompt_value_part = value_total[:prompt_count]
    resp_key_part = key_total[prompt_count:][None]
    resp_value_part = value_total[prompt_count:][None]
    prompt_key_sum, prompt_value_sum = (
        lax.psum_scatter(prompt_key_part, ("ctx", "resp"), scatter_dimension=0, tiled=True),
        lax.psum_scatter(prompt_value_part, ("ctx", "resp"), scatter_dimension=0, tiled=True),
    )
    resp_key_sum, resp_value_sum = (
        lax.psum_scatter(
            resp_key_part.astype(jnp.bfloat16), "ctx", scatter_dimension=1, tiled=True
        ).astype(jnp.float32),
        lax.psum_scatter(
            resp_value_part.astype(jnp.bfloat16), "ctx", scatter_dimension=1, tiled=True
        ).astype(jnp.float32),
    )
    return (
        grad_queries,
        resp_key_sum.astype(jnp.bfloat16),
        resp_value_sum.astype(jnp.bfloat16),
        prompt_key_sum.astype(jnp.bfloat16),
        prompt_value_sum.astype(jnp.bfloat16),
    )


def solution(mesh):
    return jax.shard_map(
        on_device,
        mesh=mesh,
        in_specs=(
            P("resp", "ctx", "head", None),
            P("resp", "ctx", "head", None),
            P("resp", "ctx", "head", None),
            P("resp", "ctx", "head", None),
            P("ctx", "head", None),
            P("ctx", "head", None),
            P("resp"),
        ),
        out_specs=(
            P("resp", "ctx", "head", None),
            P("resp", "ctx", "head", None),
            P("resp", "ctx", "head", None),
            P(("ctx", "resp"), "head", None),
            P(("ctx", "resp"), "head", None),
        ),
        check_vma=False,
    )
```

profile of v0, /device:TPU:1, one launch (start us, length us, event | category | flops | bytes accessed | tf_op | source)
XLA Modules:
  0.0 1028.5 jit_solution(10389746670971819083)
XLA Ops:
  13.7 22.5 %all_gather.15 = bf16[1,768,4,128]{3,1,2,0:T(8,128)(2,1)S(1)} all-gather(bf16[1,192,4,128]{3,1,2,0:T(8,128)(2,1)S(1)} %copy.27), channel_id=1, replica_groups=mesh['ctx'=4,'resp'=32,'head'=2] {'ctx'}, dimensions={1}, use_global_device_ids=true | all-gather | bytes 983040 | tf_op jit(solution)/shard_map/all_gather | solution.py:52
  36.2 29.0 %all_gather.13 = bf16[1,768,4,128]{3,1,2,0:T(8,128)(2,1)S(1)} all-gather(bf16[1,192,4,128]{3,1,2,0:T(8,128)(2,1)S(1)} %copy.24), channel_id=1, replica_groups=mesh['ctx'=4,'resp'=32,'head'=2] {'ctx'}, dimensions={1}, use_global_device_ids=true | all-gather | bytes 983040 | tf_op jit(solution)/shard_map/all_gather | solution.py:51
  74.7 7.0 fusion.178
  81.7 6.3 fusion.175
  88.0 4.8 convolution_bitcast_fusion.3
  92.8 6.1 convolution_bitcast_fusion.2
  99.0 6.8 fusion.172
  105.7 5.9 convolution_bitcast_fusion.1
  111.6 6.7 fusion.169
  118.3 15.8 %convolution_bitcast_fusion = f32[2304,1,128]{2,0,1:T(8,128)} fusion(bf16[192,16,128]{2,0,1:T(8,128)(2,1)S(1)} %bitcast_select_fusion.8, f32[4,192]{1,0:T(4,128)S(1)} %get-tuple-element.21, pred[192,2304]{1,0:T(8,128)(4,1)} %and_or_fusion, bf16[2304,128,1]{1,0,2:T(8,128)(2,1)} %get-tuple-element.19, bf16[192,16,128]{2,0,1:T(8,128)(2,1)} %bitcast.263), kind=kOutput, calls=%fused_computation.42 | convolution fusion | flops 914820096 | bytes 2609152 | tf_op jit(solution)/shard_map/qtj,tqd->jd/dot_general | solution.py:35
  139.7 4.9 fusion.72
  144.6 16.6 %convolution_bitcast_fusion.7 = f32[2304,1,128]{2,0,1:T(8,128)} fusion(f32[2304,192,4]{0,1,2:T(8,128)} %fusion.72, bf16[192,16,128]{2,0,1:T(8,128)(2,1)} %bitcast.264, f32[4,192,2304]{2,1,0:T(8,128)} %get-tuple-element.28, f32[4,192]{1,0:T(4,128)S(1)} %get-tuple-element.27), kind=kOutput, calls=%fused_computation.49 | convolution fusion | flops 465374208 | bytes 29696000 | tf_op jit(solution)/shard_map/qtj,tqd->jd/dot_general | solution.py:32
  161.1 3.9 fusion.76
  165.1 16.2 %convolution_bitcast_fusion.6 = f32[2304,1,128]{2,0,1:T(8,128)} fusion(f32[2304,192,4]{0,1,2:T(8,128)} %fusion.76, bf16[192,16,128]{2,0,1:T(8,128)(2,1)} %bitcast.265, f32[4,192,2304]{2,1,0:T(8,128)} %get-tuple-element.26, f32[4,192]{1,0:T(4,128)S(1)} %get-tuple-element.25), kind=kOutput, calls=%fused_computation.48 | convolution fusion | flops 465374208 | bytes 29696000 | tf_op jit(solution)/shard_map/qtj,tqd->jd/dot_general | solution.py:32
  185.2 16.6 %convolution_bitcast_fusion.5 = f32[2304,1,128]{2,0,1:T(8,128)} fusion(f32[2304,192,4]{0,1,2:T(8,128)} %fusion.68, bf16[192,16,128]{2,0,1:T(8,128)(2,1)} %bitcast.266, f32[4,192,2304]{2,1,0:T(8,128)} %get-tuple-element.24, f32[4,192]{1,0:T(4,128)S(1)} %get-tuple-element.23), kind=kOutput, calls=%fused_computation.47 | convolution fusion | flops 465374208 | bytes 29696000 | tf_op jit(solution)/shard_map/qtj,tqd->jd/dot_general | solution.py:32
  203.6 7.7 copy.30
  211.3 3.9 fusion.85
  215.2 16.2 %convolution_bitcast_fusion.4 = f32[2304,1,128]{2,0,1:T(8,128)} fusion(f32[2304,192,4]{0,1,2:T(8,128)} %fusion.85, bf16[192,16,128]{2,0,1:T(8,128)(2,1)} %bitcast.267, f32[4,192,2304]{2,1,0:T(8,128)} %get-tuple-element.22, f32[4,192]{1,0:T(4,128)S(1)} %get-tuple-element.21), kind=kOutput, calls=%fused_computation.46 | convolution fusion | flops 465374208 | bytes 29696000 | tf_op jit(solution)/shard_map/qtj,tqd->jd/dot_general | solution.py:32
  233.2 7.9 copy.29
  242.2 729.0 %all-reduce.4 = (bf16[1536,4,128]{2,1,0:T(4,128)(2,1)}, bf16[1536,4,128]{2,1,0:T(4,128)(2,1)}) all-reduce(f32[1536,4,128]{2,1,0:T(4,128)} %copy.29, f32[1536,4,128]{2,1,0:T(4,128)S(1)} %copy-done.2), channel_id=4, replica_groups=mesh['ctx'=4,'resp'=32,'head'=2] {'ctx','resp'}, use_global_device_ids=true, to_apply=%region_14.15.clone | all-reduce | flops 1572864 | bytes 9437184
  971.1 11.0 %fusion.60 = bf16[1,192,4,128]{3,1,2,0:T(8,128)(2,1)S(1)} fusion(bf16[2304,128,1]{1,0,2:T(8,128)(2,1)} %get-tuple-element.17, f32[2304,192,4]{0,1,2:T(8,128)} %fusion.72, f32[4,192,2304]{2,1,0:T(8,128)} %get-tuple-element.28, f32[4,192]{1,0:T(4,128)S(1)} %get-tuple-element.27), kind=kOutput, calls=%fused_computation.101 | convolution fusion | flops 465472512 | bytes 14945280 | tf_op jit(solution)/shard_map/qtj,jd->tqd/dot_general | solution.py:29
  982.1 10.6 %fusion.61 = bf16[1,192,4,128]{3,1,2,0:T(8,128)(2,1)S(1)} fusion(bf16[2304,128,1]{1,0,2:T(8,128)(2,1)S(1)} %copy-done.10, f32[2304,192,4]{0,1,2:T(8,128)} %fusion.76, f32[4,192,2304]{2,1,0:T(8,128)} %get-tuple-element.26, f32[4,192]{1,0:T(4,128)S(1)} %get-tuple-element.25), kind=kOutput, calls=%fused_computation.102 | convolution fusion | flops 465472512 | bytes 14945280 | tf_op jit(solution)/shard_map/qtj,jd->tqd/dot_general | solution.py:29
  992.7 10.7 %fusion.62 = bf16[1,192,4,128]{3,1,2,0:T(8,128)(2,1)S(1)} fusion(bf16[2304,128,1]{1,0,2:T(8,128)(2,1)S(1)} %copy-done.8, f32[2304,192,4]{0,1,2:T(8,128)} %fusion.68, f32[4,192,2304]{2,1,0:T(8,128)} %get-tuple-element.24, f32[4,192]{1,0:T(4,128)S(1)} %get-tuple-element.23), kind=kOutput, calls=%fused_computation.103 | convolution fusion | flops 465472512 | bytes 14945280 | tf_op jit(solution)/shard_map/qtj,jd->tqd/dot_general | solution.py:29
  1003.4 10.5 %fusion.63 = bf16[1,192,4,128]{3,1,2,0:T(8,128)(2,1)S(1)} fusion(bf16[2304,128,1]{1,0,2:T(8,128)(2,1)S(1)} %copy-done.7, f32[2304,192,4]{0,1,2:T(8,128)} %fusion.85, f32[4,192,2304]{2,1,0:T(8,128)} %get-tuple-element.22, f32[4,192]{1,0:T(4,128)S(1)} %get-tuple-element.21), kind=kOutput, calls=%fused_computation.104 | convolution fusion | flops 465472512 | bytes 14945280 | tf_op jit(solution)/shard_map/qtj,jd->tqd/dot_general | solution.py:29
  (63 shorter events, 36.4 us)
Async XLA Ops:
  7.2 62.2 %copy-start.6 = (bf16[1,192,16,128]{3,2,1,0:T(8,128)(2,1)S(1)}, bf16[1,192,16,128]{3,2,1,0:T(8,128)(2,1)}, u32[]{:S(2)}) copy-start(bf16[1,192,16,128]{3,2,1,0:T(8,128)(2,1)} %param.8) | copy-start | bytes 2359300
  7.2 65.0 %all-gather.3.cloned.1.call-start = ((), (), s32[]{:S(2)}) async-start(), calls=%async_computation.2 | async-start | bytes 1966080 | tf_op jit(solution)/shard_map/all_gather | solution.py:47
  9.2 130.5 %all-gather.5.cloned.1.call-start = ((), (), s32[]{:S(2)}) async-start(), calls=%async_computation.3 | async-start | bytes 1966080 | tf_op jit(solution)/shard_map/all_gather | solution.py:48
  11.0 1007.0 %reduce-scatter.5.cloned.1.call-start = ((), (), s32[]{:S(2)}) async-start(), calls=%async_computation.5 | async-start | bytes 983040 | tf_op jit(solution)/shard_map/reduce_scatter | solution.py:97
  74.7 13.3 %copy-start.9 = (bf16[2304,128,1]{1,0,2:T(8,128)(2,1)}, bf16[2304,128,1]{1,0,2:T(8,128)(2,1)S(1)}, u32[]{:S(2)}) copy-start(bf16[2304,128,1]{1,0,2:T(8,128)(2,1)S(1)} %get-tuple-element.18) | copy-start | bytes 1769476
  74.7 7.0 copy-start.11
  136.5 2.1 copy-start.1
  139.6 880.2 %reduce-scatter.3.cloned.1.call-start = ((), (), s32[]{:S(2)}) async-start(), calls=%async_computation.4 | async-start | bytes 983040 | tf_op jit(solution)/shard_map/reduce_scatter | solution.py:94
  144.6 16.6 %copy-start = (bf16[1536,4,128]{2,0,1:T(8,128)(2,1)S(1)}, bf16[1536,4,128]{2,0,1:T(8,128)(2,1)}, u32[]{:S(2)}) copy-start(bf16[1536,4,128]{2,0,1:T(8,128)(2,1)} %all-gather.5.cloned.1.call-done) | copy-start | bytes 4718596
  201.7 1.9 slice-start
  215.2 16.2 %copy-start.3 = (f32[2304,1,128]{2,0,1:T(8,128)S(1)}, f32[2304,1,128]{2,0,1:T(8,128)}, u32[]{:S(2)}) copy-start(f32[2304,1,128]{2,0,1:T(8,128)} %convolution_bitcast_fusion.7) | copy-start | bytes 3538948
  215.2 16.2 %copy-start.4 = (f32[2304,1,128]{2,0,1:T(8,128)S(1)}, f32[2304,1,128]{2,0,1:T(8,128)}, u32[]{:S(2)}) copy-start(f32[2304,1,128]{2,0,1:T(8,128)} %convolution_bitcast_fusion.6) | copy-start | bytes 3538948
  215.2 16.2 %copy-start.5 = (f32[2304,1,128]{2,0,1:T(8,128)S(1)}, f32[2304,1,128]{2,0,1:T(8,128)}, u32[]{:S(2)}) copy-start(f32[2304,1,128]{2,0,1:T(8,128)} %convolution_bitcast_fusion.5) | copy-start | bytes 3538948
  233.0 9.1 copy-start.2
  971.1 11.0 %copy-start.10 = (bf16[2304,128,1]{1,0,2:T(8,128)(2,1)S(1)}, bf16[2304,128,1]{1,0,2:T(8,128)(2,1)}, u32[]{:S(2)}) copy-start(bf16[2304,128,1]{1,0,2:T(8,128)(2,1)} %copy-done.9) | copy-start | bytes 1769476
  982.1 10.6 %copy-start.8 = (bf16[2304,128,1]{1,0,2:T(8,128)(2,1)S(1)}, bf16[2304,128,1]{1,0,2:T(8,128)(2,1)}, u32[]{:S(2)}) copy-start(bf16[2304,128,1]{1,0,2:T(8,128)(2,1)} %get-tuple-element.20) | copy-start | bytes 1769476
  992.7 10.7 %copy-start.7 = (bf16[2304,128,1]{1,0,2:T(8,128)(2,1)S(1)}, bf16[2304,128,1]{1,0,2:T(8,128)(2,1)}, u32[]{:S(2)}) copy-start(bf16[2304,128,1]{1,0,2:T(8,128)(2,1)} %get-tuple-element.19) | copy-start | bytes 1769476
Sparse Core Ops, SparseCore 0:
  9.8 62.2 all-gather.2
  74.0 41.6 all-gather.4
  139.7 30.9 reduce-scatter.4
  242.3 32.6 reduce-scatter.2
where the time goes:
time: 1040 us; the launch traced here: 1030 us
  blocking collectives  780 us (75%)
  matrix products  184 us (18%)
  local copies, waits for them, and re-layouts  38.4 us (4%)
  between operations  15.7 us (2%)
    unnamed x1, blocking collectives  729 us
    dot_general x4, matrix products, local_group(): jnp.einsum('qtj,tqd->jd', grad_scores, query_group, preferred_element_typ...  65.5 us
    dot_general x4, matrix products, local_group(): jnp.einsum('qtj,jd->tqd', grad_scores, key_group, preferred_element_type=...  42.7 us
    dot_general x4, matrix products, local_group(): jnp.einsum('qtj,tqd->jd', weights_low, grad_group, preferred_element_type...  32.6 us
    all_gather x1, blocking collectives, on_device(): lax.all_gather(resp_keys, 'ctx', axis=1, tiled=True)  29 us
    sub x4, matrix products, local_group(): exponent = jnp.exp(scores - row_max)  26.8 us
    all_gather x1, blocking collectives, on_device(): lax.all_gather(resp_values, 'ctx', axis=1, tiled=True)  22.5 us
  transfers between devices with their start and end apart: 4, of which 1 were waited for; matrix products, arithmetic and copies ran while one was open for 22% of the time, Pallas kernels for 0%

commit v1 on v0

v1 whole, which is shorter than its diff:
```python
import functools

import jax
import jax.numpy as jnp
from jax import lax
from jax.experimental import pallas as pl
from jax.experimental.pallas import tpu as pltpu
from jax.sharding import PartitionSpec as P

F32 = jnp.float32
BF16 = jnp.bfloat16
MESH = pl.DeviceIdType.MESH
SCALE = 128 ** -0.5
LOG2E = 1.4426950408889634
CEXP = SCALE * LOG2E
NG = 4
NC = 4
ROWS = 192
PROWS = 384
QROWS = 768
BLK = 384
NPB = 4
NRB = 2
PIECE = 96
LOW = -1e30


def matmul(a, b):
    return lax.dot_general(a, b, (((1,), (0,)), ((), ())), preferred_element_type=F32)


def matmul_t(a, b):
    return lax.dot_general(a, b, (((0,), (0,)), ((), ())), preferred_element_type=F32)


def kernel(
    q_hbm, do_hbm, rk_hbm, rv_hbm, pk_hbm, pv_hbm, len_ref,
    dq_out, drk_out, drv_out, dpk_out, dpv_out,
    q_raw, do_raw, rk_raw, rv_raw, pk_raw, pv_raw,
    tmp, pkv, rkv, qs, dos, e_s, w_s, m_s, d_prompt, d_resp, dq_s,
    s1, r1, s2, r2, s3, r3, sp, rp, fin_r, fin_p,
    in_sem,
    z_send, z_recv, x_send, x_recv, c_send, c_recv, k_send, k_recv,
    a_send, a_recv, b_send, b_recv, o_send, o_recv, p_send, p_recv,
):
    ctx = lax.axis_index("ctx")
    resp = lax.axis_index("resp")
    core = resp % 2
    chip = resp // 2
    cx = chip // 4
    cy = chip % 4
    other = resp + 1 - 2 * core
    is_self = (cx == 0) & (cy == 0)

    def remote(src, dst, send, recv, to):
        return pltpu.make_async_remote_copy(
            src_ref=src, dst_ref=dst, send_sem=send, recv_sem=recv,
            device_id=to, device_id_type=MESH,
        )

    def ctx_at(d):
        return (ctx + d) % NC

    def plane_at(d):
        return ((chip + d) % 16) * 2 + core

    def owner(chunk, half):
        return {"ctx": (ctx + cx) % NC, "resp": (cy * 4 + chunk) * 2 + half}

    def source(sx, kind):
        return {"ctx": (ctx + NC - sx) % NC, "resp": (sx * 4 + cx) * 2 + kind}

    barrier = pltpu.get_barrier_semaphore()

    def greet(to):
        pl.semaphore_signal(barrier, inc=1, device_id=to, device_id_type=MESH)

    loads = []
    for i, (src, dst) in enumerate(
        ((pk_hbm, pk_raw), (pv_hbm, pv_raw), (rk_hbm, rk_raw), (rv_hbm, rv_raw), (q_hbm, q_raw), (do_hbm, do_raw))
    ):
        load = pltpu.make_async_copy(src, dst, in_sem.at[i])
        load.start()
        loads.append(load)

    for d in range(1, NC):
        greet({"ctx": ctx_at(d)})

    def greet_plane(d, _):
        greet({"resp": plane_at(d)})
        return 0

    lax.fori_loop(1, 16, greet_plane, 0)
    greet({"resp": other})
    for a in range(4):
        for h in range(2):
            own_to = is_self & (core == h) if a == 0 else False

            def greet_pair(a=a, h=h):
                greet(owner(a, h))
                greet(source(a, h))

            if a == 0:
                pl.when(jnp.logical_not(own_to))(greet_pair)
            else:
                greet_pair()

    for b in range(1, NC):
        @pl.when(ctx < b)
        def _(b=b):
            for kind in range(2):
                for g in range(NG):
                    rkv[kind, g, b] = jnp.zeros((ROWS, 128), BF16)

    for kind in range(2):
        loads[kind].wait()
        raw = pk_raw if kind == 0 else pv_raw
        tmp[0 : PROWS * NG, :] = raw[...].astype(F32)
        for g in range(NG):
            pkv[kind, g, 0] = tmp[pl.ds(g, PROWS, stride=NG), :].astype(BF16).reshape(4, PIECE, 128)
    for kind in range(2):
        loads[2 + kind].wait()
        raw = rk_raw if kind == 0 else rv_raw
        tmp[0 : ROWS * NG, :] = raw[...].astype(F32)
        for g in range(NG):
            rkv[kind, g, ctx] = tmp[pl.ds(g, ROWS, stride=NG), :].astype(BF16)

    @pl.when(is_self)
    def _():
        pl.semaphore_wait(barrier, 33)

    @pl.when(jnp.logical_not(is_self))
    def _():
        pl.semaphore_wait(barrier, 35)

    def z_copy(g, d):
        return remote(
            pkv.at[core, g, 0, cx], pkv.at[core, g, NC - d, cx],
            z_send.at[g, d - 1], z_recv.at[g, NC - d - 1], {"ctx": ctx_at(d)},
        )

    def z_arrival(g, d):
        return remote(
            pkv.at[core, g, 0, cx], pkv.at[core, g, d, cx],
            z_send.at[g, d - 1], z_recv.at[g, d - 1], {"ctx": ctx_at(d)},
        )

    def x_copy(g, d):
        to = ((cx + d) % 4 * 4 + cy) * 2 + core
        return remote(
            pkv.at[core, g, pl.ds(1, 3), cx], pkv.at[core, g, pl.ds(1, 3), cx],
            x_send.at[g, d - 1], x_recv.at[g, d - 1], {"resp": to},
        )

    def x_arrival(g, d):
        sx = (cx + 4 - d) % 4
        to = ((cx + d) % 4 * 4 + cy) * 2 + core
        return remote(
            pkv.at[core, g, pl.ds(1, 3), sx], pkv.at[core, g, pl.ds(1, 3), sx],
            x_send.at[g, d - 1], x_recv.at[g, d - 1], {"resp": to},
        )

    def c_copy(g):
        return remote(
            pkv.at[core, g, pl.ds(1, 3)], pkv.at[core, g, pl.ds(1, 3)],
            c_send.at[g], c_recv.at[g], {"resp": other},
        )

    def c_arrival(g):
        return remote(
            pkv.at[1 - core, g, pl.ds(1, 3)], pkv.at[1 - core, g, pl.ds(1, 3)],
            c_send.at[g], c_recv.at[g], {"resp": other},
        )

    def k_copy(g, kind, to):
        return remote(
            rkv.at[kind, g, ctx], rkv.at[kind, g, ctx],
            k_send.at[g, kind, to], k_recv.at[g, kind, ctx], {"ctx": to},
        )

    def k_arrival(g, kind, src):
        return remote(
            rkv.at[kind, g, src], rkv.at[kind, g, src],
            k_send.at[g, kind, src], k_recv.at[g, kind, src], {"ctx": src},
        )

    def a_copy(g):
        return remote(s1.at[g], r1.at[g], a_send.at[g], a_recv.at[g], {"resp": other})

    def b_copy(g, d):
        to = (chip + d) % 16
        return remote(
            s2.at[g, to], r2.at[g, chip], b_send.at[g, d], b_recv.at[g, d], {"resp": to * 2 + core},
        )

    def b_arrival(g, d):
        src = (chip + 16 - d) % 16
        return remote(
            s2.at[g, src], r2.at[g, src], b_send.at[g, d], b_recv.at[g, d], {"resp": src * 2 + core},
        )

    def o_copy(g, chunk, half):
        return remote(
            s3.at[g, pl.ds(chunk * 24 + half * 8, 16)], r3.at[g, core, cx],
            o_send.at[g, chunk, half], o_recv.at[g, core, cx], owner(chunk, half),
        )

    def o_arrival(g, sx, kind):
        return remote(
            s3.at[g, pl.ds(0, 16)], r3.at[g, kind, sx],
            o_send.at[g, sx, kind], o_recv.at[g, kind, sx], source(sx, kind),
        )

    def p_copy(g, kind, to):
        return remote(
            sp.at[kind, g, to], rp.at[kind, g, ctx],
            p_send.at[g, kind, to], p_recv.at[g, kind, ctx], {"ctx": to},
        )

    def p_arrival(g, kind, src):
        return remote(
            sp.at[kind, g, src], rp.at[kind, g, src],
            p_send.at[g, kind, src], p_recv.at[g, kind, src], {"ctx": src},
        )

    def each_above(body):
        for c in range(1, NC):
            @pl.when(ctx < c)
            def _(c=c):
                for kind in range(2):
                    body(kind, c)

    def each_below(body):
        for c in range(NC - 1):
            @pl.when(ctx > c)
            def _(c=c):
                for kind in range(2):
                    body(kind, c)

    def send_first(g, _):
        for d in range(1, NC):
            z_copy(g, d).start()
        each_above(lambda kind, c: k_copy(g, kind, c).start())
        return 0

    lax.fori_loop(0, NG, send_first, 0)

    def forward_x(g):
        for d in range(1, NC):
            z_arrival(g, d).wait_recv()
        for d in range(1, NC):
            x_copy(g, d).start()

    def forward_core(g):
        for d in range(1, NC):
            x_arrival(g, d).wait_recv()
        c_copy(g).start()

    length = len_ref[0]
    first = ctx * ROWS

    def take_heads(load, raw, dst, keep):
        load.wait()
        tmp[...] = raw[...].astype(F32)
        for h in range(16):
            rows = tmp[pl.ds(h, ROWS, stride=16), :]
            if keep is not None:
                rows = jnp.where(keep, rows, 0.0)
            dst[h // 4, (h % 4) * ROWS : (h % 4 + 1) * ROWS, :] = rows.astype(BF16)

    take_heads(loads[4], q_raw, qs, None)
    forward_x(0)
    position = first + lax.broadcasted_iota(jnp.int32, (ROWS, 128), 0)
    take_heads(loads[5], do_raw, dos, position < length)
    forward_core(0)

    def key_block(g, kind, j):
        if j < NPB:
            return pkv[kind, g, j].reshape(BLK, 128)
        b = j - NPB
        return rkv[kind, g, 2 * b : 2 * b + 2].reshape(BLK, 128)

    def plane_send(g):
        a_copy(g).wait_recv()
        total = d_prompt[core] + r1[g].astype(F32)
        s2[g] = total.astype(BF16).reshape(16, PIECE, 128)

        def send(d, _):
            b_copy(g, d).start()
            return 0

        lax.fori_loop(1, 16, send, 0)

    def owner_send(g):
        def wait(d, _):
            b_arrival(g, d).wait_recv()
            return 0

        lax.fori_loop(1, 16, wait, 0)
        r2[g, chip] = s2[g, chip]
        total = r2[g, 0].astype(F32)
        for i in range(1, 16):
            total = total + r2[g, i].astype(F32)
        s3[g] = total * jnp.where(core == 0, SCALE, 1.0)
        for chunk in range(4):
            for half in range(2):
                if chunk == 0:
                    mine = is_self & (core == half)

                    @pl.when(mine)
                    def _(half=half):
                        r3[g, core, cx] = s3[g, half * 8 : half * 8 + 16, :]

                    @pl.when(jnp.logical_not(mine))
                    def _(half=half):
                        o_copy(g, 0, half).start()
                else:
                    o_copy(g, chunk, half).start()

    def group(g, _):
        each_below(lambda kind, c: k_arrival(g, kind, c).wait_recv())
        c_arrival(g).wait_recv()
        q = qs[g]
        do = dos[g]
        qt = q.T
        dot = do.T
        high = jnp.full((1, QROWS), LOW, F32)
        norm = jnp.zeros((1, QROWS), F32)
        delta = jnp.zeros((1, QROWS), F32)
        for j in range(NPB + NRB):
            keys = slice(j * BLK, (j + 1) * BLK)
            s = matmul(key_block(g, 0, j), qt)
            w = matmul(key_block(g, 1, j), dot)
            w_s[keys, :] = w
            if j >= NPB:
                r = lax.broadcasted_iota(jnp.int32, (BLK, QROWS), 0) + (j - NPB) * BLK
                t = lax.broadcasted_iota(jnp.int32, (1, QROWS), 1) % ROWS + first
                s = jnp.where(r <= t, s, LOW)
            new = jnp.maximum(high, jnp.max(s, axis=0, keepdims=True))
            e = jnp.exp2((s - new) * CEXP)
            e_s[keys, :] = e
            m_s[j, 0:1, :] = new
            fix = jnp.exp2((high - new) * CEXP)
            norm = norm * fix + jnp.sum(e, axis=0, keepdims=True)
            delta = delta * fix + jnp.sum(e * w, axis=0, keepdims=True)
            high = new
        inverse = 1.0 / norm
        delta = delta * inverse

        @pl.when(g < NG - 1)
        def _():
            forward_x(g + 1)

        @pl.when(g >= 1)
        def _():
            plane_send(g - 1)

        dq = jnp.zeros((128, QROWS), F32)
        for j in range(NPB + NRB):
            keys = slice(j * BLK, (j + 1) * BLK)
            weight = jnp.exp2((m_s[j, 0:1, :] - high) * CEXP) * inverse
            p = e_s[keys, :] * weight
            ds = (p * (w_s[keys, :] - delta)).astype(BF16)
            dv = matmul(p.astype(BF16), do)
            dk = matmul(ds, q)
            if j < NPB:
                d_prompt[0, keys, :] = dk
                d_prompt[1, keys, :] = dv
            else:
                b = 2 * (j - NPB)
                sp[0, g, b : b + 2] = (dk * SCALE).astype(BF16).reshape(2, ROWS, 128)
                sp[1, g, b : b + 2] = dv.astype(BF16).reshape(2, ROWS, 128)
            dq = dq + matmul_t(key_block(g, 0, j), ds)
        s1[g] = d_prompt[1 - core].astype(BF16)
        a_copy(g).start()
        each_below(lambda kind, c: p_copy(g, kind, c).start())
        dq = dq.T * SCALE
        for i in range(4):
            dq_s[pl.ds(g * 4 + i, ROWS, stride=16), :] = dq[i * ROWS : (i + 1) * ROWS, :]

        @pl.when(g < NG - 1)
        def _():
            forward_core(g + 1)

        @pl.when(g >= 1)
        def _():
            owner_send(g - 1)

        return 0

    lax.fori_loop(0, NG, group, 0)
    plane_send(NG - 1)
    dq_out[...] = dq_s[...].astype(BF16)

    def resp_wait(g, _):
        each_above(lambda kind, c: p_arrival(g, kind, c).wait_recv())
        return 0

    lax.fori_loop(0, NG, resp_wait, 0)
    for c in range(1, NC):
        @pl.when(ctx >= c)
        def _(c=c):
            for kind in range(2):
                for g in range(NG):
                    rp[kind, g, c] = jnp.zeros((ROWS, 128), BF16)

    for kind in range(2):
        for g in range(NG):
            total = sp[kind, g, ctx].astype(F32)
            for c in range(1, NC):
                total = total + rp[kind, g, c].astype(F32)
            fin_r[pl.ds(g, ROWS, stride=NG), :] = total
        out = drk_out if kind == 0 else drv_out
        out[...] = fin_r[...].astype(BF16)

    owner_send(NG - 1)

    def owner_wait(g, _):
        for sx in range(4):
            for kind in range(2):
                if sx == 0:
                    @pl.when(jnp.logical_not(is_self & (core == kind)))
                    def _(kind=kind):
                        o_arrival(g, 0, kind).wait_recv()
                else:
                    o_arrival(g, sx, kind).wait_recv()
        return 0

    lax.fori_loop(0, NG, owner_wait, 0)
    for kind in range(2):
        for g in range(NG):
            total = (r3[g, kind, 0] + r3[g, kind, 1]) + (r3[g, kind, 2] + r3[g, kind, 3])
            fin_p[pl.ds(g, 12, stride=NG), :] = jnp.where(core == 0, total[0:12], total[4:16])
        out = dpk_out if kind == 0 else dpv_out
        out[...] = fin_p[...].astype(BF16)

    def sent(g, _):
        for d in range(1, NC):
            z_copy(g, d).wait_send()
            x_copy(g, d).wait_send()
        c_copy(g).wait_send()
        a_copy(g).wait_send()
        each_above(lambda kind, c: k_copy(g, kind, c).wait_send())
        each_below(lambda kind, c: p_copy(g, kind, c).wait_send())

        def sent_plane(d, _):
            b_copy(g, d).wait_send()
            return 0

        lax.fori_loop(1, 16, sent_plane, 0)
        for chunk in range(4):
            for half in range(2):
                if chunk == 0:
                    @pl.when(jnp.logical_not(is_self & (core == half)))
                    def _(half=half):
                        o_copy(g, 0, half).wait_send()
                else:
                    o_copy(g, chunk, half).wait_send()
        return 0

    lax.fori_loop(0, NG, sent, 0)


def on_device(queries, grad_out, resp_keys, resp_values, prompt_keys, prompt_values, resp_lengths):
    dma = pltpu.SemaphoreType.DMA
    vmem = pltpu.VMEM
    outs = pl.pallas_call(
        kernel,
        out_shape=[
            jax.ShapeDtypeStruct((ROWS * 16, 128), BF16),
            jax.ShapeDtypeStruct((ROWS * NG, 128), BF16),
            jax.ShapeDtypeStruct((ROWS * NG, 128), BF16),
            jax.ShapeDtypeStruct((12 * NG, 128), BF16),
            jax.ShapeDtypeStruct((12 * NG, 128), BF16),
        ],
        in_specs=[pl.BlockSpec(memory_space=pl.ANY)] * 6 + [pl.BlockSpec(memory_space=pltpu.SMEM)],
        out_specs=[pl.BlockSpec(memory_space=pltpu.VMEM)] * 5,
        scratch_shapes=[
            vmem((ROWS * 16, 128), BF16),
            vmem((ROWS * 16, 128), BF16),
            vmem((ROWS * NG, 128), BF16),
            vmem((ROWS * NG, 128), BF16),
            vmem((PROWS * NG, 128), BF16),
            vmem((PROWS * NG, 128), BF16),
            vmem((ROWS * 16, 128), F32),
            vmem((2, NG, 4, 4, PIECE, 128), BF16),
            vmem((2, NG, NC, ROWS, 128), BF16),
            vmem((NG, QROWS, 128), BF16),
            vmem((NG, QROWS, 128), BF16),
            vmem(((NPB + NRB) * BLK, QROWS), F32),
            vmem(((NPB + NRB) * BLK, QROWS), F32),
            vmem((NPB + NRB, 8, QROWS), F32),
            vmem((2, NPB * BLK, 128), F32),
            vmem((8, 128), F32),
            vmem((ROWS * 16, 128), F32),
            vmem((NG, NPB * BLK, 128), BF16),
            vmem((NG, NPB * BLK, 128), BF16),
            vmem((NG, 16, PIECE, 128), BF16),
            vmem((NG, 16, PIECE, 128), BF16),
            vmem((NG, PIECE, 128), F32),
            vmem((NG, 2, 4, 16, 128), F32),
            vmem((2, NG, NC, ROWS, 128), BF16),
            vmem((2, NG, NC, ROWS, 128), BF16),
            vmem((ROWS * NG, 128), F32),
            vmem((12 * NG, 128), F32),
            dma((6,)),
            dma((NG, 3)), dma((NG, 3)),
            dma((NG, 3)), dma((NG, 3)),
            dma((NG,)), dma((NG,)),
            dma((NG, 2, NC)), dma((NG, 2, NC)),
            dma((NG,)), dma((NG,)),
            dma((NG, 16)), dma((NG, 16)),
            dma((NG, 4, 2)), dma((NG, 2, 4)),
            dma((NG, 2, NC)), dma((NG, 2, NC)),
        ],
        compiler_params=pltpu.CompilerParams(
            collective_id=0, has_side_effects=True, vmem_limit_bytes=56 * 1024 * 1024,
        ),
        name="attention_backward",
    )(
        queries.reshape(ROWS * 16, 128),
        grad_out.reshape(ROWS * 16, 128),
        resp_keys.reshape(ROWS * NG, 128),
        resp_values.reshape(ROWS * NG, 128),
        prompt_keys.reshape(PROWS * NG, 128),
        prompt_values.reshape(PROWS * NG, 128),
        resp_lengths,
    )
    return (
        outs[0].reshape(queries.shape),
        outs[1].reshape(resp_keys.shape),
        outs[2].reshape(resp_values.shape),
        outs[3].reshape(12, NG, 128),
        outs[4].reshape(12, NG, 128),
    )


def solution(mesh):
    heads = P("resp", "ctx", "head", None)
    prompt = P("ctx", "head", None)
    owners = P(("ctx", "resp"), "head", None)
    return jax.shard_map(
        on_device,
        mesh=mesh,
        in_specs=(heads, heads, heads, heads, prompt, prompt, P("resp")),
        out_specs=(heads, heads, heads, owners, owners),
        check_vma=False,
    )
```

time: 1040 us -> 102 us (0.10)
  blocking collectives: 780 us -> 0 us
  matrix products: 184 us -> 0 us
  Pallas kernels: 0 us -> 94.4 us
  local copies, waits for them, and re-layouts: 38.4 us -> 5.2 us
  between operations: 15.7 us -> 1.3 us
    unnamed x1 -> x0, blocking collectives: 729 us -> none
    dot_general x16 -> x0, matrix products: 158 us -> none  [the longest x4 65.5 us: local_group(): jnp.einsum('qtj,tqd->jd', grad_scores, query_group, preferred_element_typ...]
    pallas_call x0 -> x1, Pallas kernels: none -> 94.4 us  [on_device(): pl.pallas_call(kernel, out_shape=[jax.ShapeDtypeStruct((ROWS * 16, 128),...]
    all_gather x2 -> x0, blocking collectives: 51.5 us -> none  [the longest x1 29 us: on_device(): lax.all_gather(resp_keys, 'ctx', axis=1, tiled=True)]
    sub x4 -> x0, matrix products: 26.8 us -> none  [local_group(): exponent = jnp.exp(scores - row_max)]
    slice x5 -> x0, local copies, waits for them, and re-layouts: 17.6 us -> none  [the longest x3 9.55 us: on_device(): prompt_value_part = value_total[:prompt_count]]
    unnamed x33 -> x13, local copies, waits for them, and re-layouts: 16.2 us -> 5.2 us
  transfers between devices with their start and end apart: 4 -> 0, of which waited for: 1 -> 0; matrix products, arithmetic and copies ran while one was open for 22% -> 0% of each run, Pallas kernels for 0% -> 0%
where the time goes in v1:
time: 102 us; the launch traced here: 101 us
  Pallas kernels  94.4 us (93%)
  local copies, waits for them, and re-layouts  5.2 us (5%)
  between operations  1.3 us (1%)
    pallas_call x1, Pallas kernels, on_device(): pl.pallas_call(kernel, out_shape=[jax.ShapeDtypeStruct((ROWS * 16, 128),...  94.4 us
    unnamed x13, local copies, waits for them, and re-layouts  5.2 us

profile of v1, /device:TPU:1, one launch (start us, length us, event | category | flops | bytes accessed | tf_op | source)
XLA Modules:
  0.0 100.9 jit_solution(8595026219336050737)
XLA Ops:
  1.3 94.4 %attention_backward.1 = (bf16[3072,128]{1,0:T(8,128)(2,1)}, bf16[768,128]{1,0:T(8,128)(2,1)}, bf16[768,128]{1,0:T(8,128)(2,1)}, bf16[48,128]{1,0:T(8,128)(2,1)}, bf16[48,128]{1,0:T(8,128)(2,1)}) custom-call(bf16[3072,128]{1,0:T(8,128)(2,1)} %bitcast.12, bf16[3072,128]{1,0:T(8,128)(2,1)} %bitcast.13, bf16[768,128]{1,0:T(8,128)(2,1)} %bitcast.16, ...), custom_call_target="tpu_custom_call" | custom-call | tf_op jit(solution)/shard_map/attention_backward/pallas_call | solution.py:467
  95.7 0.0 copy-start.1
  95.7 2.2 %copy.18 = bf16[1,192,16,128]{3,2,1,0:T(8,128)(2,1)} copy(bf16[1,192,16,128]{3,2,1,0:T(8,128)(2,1)} %bitcast.11) | data formatting | bytes 1572864
  97.9 0.0 copy-done.1
  97.9 0.0 copy-start
  97.9 0.7 copy.19
  98.6 0.3 copy-done
  98.9 0.0 copy-start.3
  98.9 0.7 copy.20
  99.6 0.0 copy-done.3
  99.6 0.0 copy-start.2
  99.6 0.6 copy.21
  100.2 0.1 copy-done.2
  100.3 0.6 copy.22
Async XLA Ops:
  95.7 2.2 %copy-start.1 = (bf16[768,128]{1,0:T(8,128)(2,1)S(1)}, bf16[768,128]{1,0:T(8,128)(2,1)}, u32[]{:S(2)}) copy-start(bf16[768,128]{1,0:T(8,128)(2,1)} %get-tuple-element.11) | copy-start | bytes 589828
  97.9 1.0 copy-start
  98.9 0.7 copy-start.3
  99.6 0.7 copy-start.2

commit v2 on v1

--- a/solution.py
+++ b/solution.py
@@ -23,6 +23,8 @@
 NRB = 2
 PIECE = 96
 LOW = -1e30
+ORDER_A = (0, 4, 5, 1, 2, 3)
+ORDER_C = (4, 5, 0, 1, 2, 3)
 
 
 def matmul(a, b):
@@ -37,11 +39,11 @@
     q_hbm, do_hbm, rk_hbm, rv_hbm, pk_hbm, pv_hbm, len_ref,
     dq_out, drk_out, drv_out, dpk_out, dpv_out,
     q_raw, do_raw, rk_raw, rv_raw, pk_raw, pv_raw,
-    tmp, pkv, rkv, qs, dos, e_s, w_s, m_s, d_prompt, d_resp, dq_s,
-    s1, r1, s2, r2, s3, r3, sp, rp, fin_r, fin_p,
+    tmp, pkv, rkv, qs, dos, e_s, w_s, m_s, dq_s,
+    s1, r1, s2, r2, s4, r4, s3, r3, sp, rp, fin_r, fin_p,
     in_sem,
     z_send, z_recv, x_send, x_recv, c_send, c_recv, k_send, k_recv,
-    a_send, a_recv, b_send, b_recv, o_send, o_recv, p_send, p_recv,
+    a_send, a_recv, b_send, b_recv, y_send, y_recv, o_send, o_recv, p_send, p_recv,
 ):
     ctx = lax.axis_index("ctx")
     resp = lax.axis_index("resp")
@@ -50,7 +52,9 @@
     cx = chip // 4
     cy = chip % 4
     other = resp + 1 - 2 * core
-    is_self = (cx == 0) & (cy == 0)
+    u = jnp.where(core == 0, cx, cy)
+    v = jnp.where(core == 0, cy, cx)
+    is_self = (u == 0) & (v == cx) & (cy == 0)
 
     def remote(src, dst, send, recv, to):
         return pltpu.make_async_remote_copy(
@@ -61,14 +65,21 @@
     def ctx_at(d):
         return (ctx + d) % NC
 
-    def plane_at(d):
-        return ((chip + d) % 16) * 2 + core
+    def plane_at(pu, pv):
+        return (pu * (4 - 3 * core) + pv * (1 + 3 * core)) * 2 + core
+
+    def u_at(d):
+        return plane_at((u + d) % 4, v)
+
+    def v_at(d):
+        return plane_at(u, (v + d) % 4)
 
     def owner(chunk, half):
-        return {"ctx": (ctx + cx) % NC, "resp": (cy * 4 + chunk) * 2 + half}
-
-    def source(sx, kind):
-        return {"ctx": (ctx + NC - sx) % NC, "resp": (sx * 4 + cx) * 2 + kind}
+        return {"ctx": (ctx + u) % NC, "resp": (v * 4 + chunk) * 2 + half}
+
+    def source(su, kind):
+        at = su * (4 - 3 * kind) + cx * (1 + 3 * kind)
+        return {"ctx": (ctx + NC - su) % NC, "resp": at * 2 + kind}
 
     barrier = pltpu.get_barrier_semaphore()
 
@@ -86,11 +97,9 @@
     for d in range(1, NC):
         greet({"ctx": ctx_at(d)})
 
-    def greet_plane(d, _):
-        greet({"resp": plane_at(d)})
-        return 0
-
-    lax.fori_loop(1, 16, greet_plane, 0)
+    for d in range(1, 4):
+        greet({"resp": u_at(d)})
+        greet({"resp": v_at(d)})
     greet({"resp": other})
     for a in range(4):
         for h in range(2):
@@ -111,6 +120,12 @@
             for kind in range(2):
                 for g in range(NG):
                     rkv[kind, g, b] = jnp.zeros((ROWS, 128), BF16)
+
+        @pl.when((ctx >= b) | ((ctx == 0) & (b == NC - 1)))
+        def _(b=b):
+            for kind in range(2):
+                for g in range(NG):
+                    rp[kind, g, b] = jnp.zeros((ROWS, 128), BF16)
 
     for kind in range(2):
         loads[kind].wait()
@@ -127,37 +142,35 @@
 
     @pl.when(is_self)
     def _():
-        pl.semaphore_wait(barrier, 33)
+        pl.semaphore_wait(barrier, 24)
 
     @pl.when(jnp.logical_not(is_self))
     def _():
-        pl.semaphore_wait(barrier, 35)
+        pl.semaphore_wait(barrier, 26)
 
     def z_copy(g, d):
         return remote(
-            pkv.at[core, g, 0, cx], pkv.at[core, g, NC - d, cx],
+            pkv.at[core, g, 0, v], pkv.at[core, g, NC - d, v],
             z_send.at[g, d - 1], z_recv.at[g, NC - d - 1], {"ctx": ctx_at(d)},
         )
 
     def z_arrival(g, d):
         return remote(
-            pkv.at[core, g, 0, cx], pkv.at[core, g, d, cx],
+            pkv.at[core, g, 0, v], pkv.at[core, g, d, v],
             z_send.at[g, d - 1], z_recv.at[g, d - 1], {"ctx": ctx_at(d)},
         )
 
     def x_copy(g, d):
-        to = ((cx + d) % 4 * 4 + cy) * 2 + core
-        return remote(
-            pkv.at[core, g, pl.ds(1, 3), cx], pkv.at[core, g, pl.ds(1, 3), cx],
-            x_send.at[g, d - 1], x_recv.at[g, d - 1], {"resp": to},
+        return remote(
+            pkv.at[core, g, pl.ds(1, 3), v], pkv.at[core, g, pl.ds(1, 3), v],
+            x_send.at[g, d - 1], x_recv.at[g, d - 1], {"resp": v_at(d)},
         )
 
     def x_arrival(g, d):
-        sx = (cx + 4 - d) % 4
-        to = ((cx + d) % 4 * 4 + cy) * 2 + core
-        return remote(
-            pkv.at[core, g, pl.ds(1, 3), sx], pkv.at[core, g, pl.ds(1, 3), sx],
-            x_send.at[g, d - 1], x_recv.at[g, d - 1], {"resp": to},
+        sv = (v + 4 - d) % 4
+        return remote(
+            pkv.at[core, g, pl.ds(1, 3), sv], pkv.at[core, g, pl.ds(1, 3), sv],
+            x_send.at[g, d - 1], x_recv.at[g, d - 1], {"resp": v_at(4 - d)},
         )
 
     def c_copy(g):
@@ -184,31 +197,53 @@
             k_send.at[g, kind, src], k_recv.at[g, kind, src], {"ctx": src},
         )
 
-    def a_copy(g):
-        return remote(s1.at[g], r1.at[g], a_send.at[g], a_recv.at[g], {"resp": other})
+    def k_onward(g, kind):
+        return remote(
+            rkv.at[kind, g, 0], rkv.at[kind, g, 0],
+            k_send.at[g, kind, 0], k_recv.at[g, kind, 0], {"ctx": 3},
+        )
+
+    def a_copy(g, j):
+        return remote(
+            s1.at[1 - core, g, j], r1.at[g, j], a_send.at[g, j], a_recv.at[g, j], {"resp": other}
+        )
 
     def b_copy(g, d):
-        to = (chip + d) % 16
-        return remote(
-            s2.at[g, to], r2.at[g, chip], b_send.at[g, d], b_recv.at[g, d], {"resp": to * 2 + core},
+        return remote(
+            s2.at[g, (u + d) % 4], r2.at[g, u],
+            b_send.at[g, d - 1], b_recv.at[g, d - 1], {"resp": u_at(d)},
         )
 
     def b_arrival(g, d):
-        src = (chip + 16 - d) % 16
-        return remote(
-            s2.at[g, src], r2.at[g, src], b_send.at[g, d], b_recv.at[g, d], {"resp": src * 2 + core},
+        src = (u + 4 - d) % 4
+        return remote(
+            s2.at[g, src], r2.at[g, src],
+            b_send.at[g, d - 1], b_recv.at[g, d - 1], {"resp": u_at(4 - d)},
+        )
+
+    def y_copy(g, d):
+        return remote(
+            s4.at[g, (v + d) % 4], r4.at[g, v],
+            y_send.at[g, d - 1], y_recv.at[g, d - 1], {"resp": v_at(d)},
+        )
+
+    def y_arrival(g, d):
+        src = (v + 4 - d) % 4
+        return remote(
+            s4.at[g, src], r4.at[g, src],
+            y_send.at[g, d - 1], y_recv.at[g, d - 1], {"resp": v_at(4 - d)},
         )
 
     def o_copy(g, chunk, half):
         return remote(
-            s3.at[g, pl.ds(chunk * 24 + half * 8, 16)], r3.at[g, core, cx],
-            o_send.at[g, chunk, half], o_recv.at[g, core, cx], owner(chunk, half),
-        )
-
-    def o_arrival(g, sx, kind):
-        return remote(
-            s3.at[g, pl.ds(0, 16)], r3.at[g, kind, sx],
-            o_send.at[g, sx, kind], o_recv.at[g, kind, sx], source(sx, kind),
+            s3.at[g, chunk, half], r3.at[g, core, u],
+            o_send.at[g, chunk, half], o_recv.at[g, core, u], owner(chunk, half),
+        )
+
+    def o_arrival(g, su, kind):
+        return remote(
+            s3.at[g, su, kind], r3.at[g, kind, su],
+            o_send.at[g, su, kind], o_recv.at[g, kind, su], source(su, kind),
         )
 
     def p_copy(g, kind, to):
@@ -223,16 +258,22 @@
             p_send.at[g, kind, src], p_recv.at[g, kind, src], {"ctx": src},
         )
 
+    def p_inward(g, kind):
+        return remote(
+            sp.at[kind, g, 0], rp.at[kind, g, 0],
+            p_send.at[g, kind, 0], p_recv.at[g, kind, 0], {"ctx": 2},
+        )
+
     def each_above(body):
         for c in range(1, NC):
-            @pl.when(ctx < c)
+            @pl.when((ctx < c) & ((ctx > 0) | (c < NC - 1)))
             def _(c=c):
                 for kind in range(2):
                     body(kind, c)
 
     def each_below(body):
         for c in range(NC - 1):
-            @pl.when(ctx > c)
+            @pl.when((ctx > c) & ((ctx < NC - 1) | (c > 0)))
             def _(c=c):
                 for kind in range(2):
                     body(kind, c)
@@ -244,6 +285,22 @@
         return 0
 
     lax.fori_loop(0, NG, send_first, 0)
+
+    def onward(g):
+        @pl.when(ctx == 2)
+        def _():
+            for kind in range(2):
+                k_arrival(g, kind, 0).wait_recv()
+                k_onward(g, kind).start()
+
+    def inward(g):
+        @pl.when(ctx == 2)
+        def _():
+            for kind in range(2):
+                p_inward(g, kind).wait_recv()
+                total = sp[kind, g, 0].astype(F32) + rp[kind, g, 0].astype(F32)
+                sp[kind, g, 0] = total.astype(BF16)
+                p_copy(g, kind, 0).start()
 
     def forward_x(g):
         for d in range(1, NC):
@@ -273,6 +330,7 @@
     position = first + lax.broadcasted_iota(jnp.int32, (ROWS, 128), 0)
     take_heads(loads[5], do_raw, dos, position < length)
     forward_core(0)
+    onward(0)
 
     def key_block(g, kind, j):
         if j < NPB:
@@ -280,28 +338,35 @@
         b = j - NPB
         return rkv[kind, g, 2 * b : 2 * b + 2].reshape(BLK, 128)
 
+    def swap_send(g):
+        for j in range(NPB):
+            a_copy(g, j).wait_recv()
+            total = s1[core, g, j].astype(F32) + r1[g, j].astype(F32)
+            s2[g, j] = total.astype(BF16).reshape(4, PIECE, 128)
+        for d in range(1, 4):
+            b_copy(g, d).start()
+
     def plane_send(g):
-        a_copy(g).wait_recv()
-        total = d_prompt[core] + r1[g].astype(F32)
-        s2[g] = total.astype(BF16).reshape(16, PIECE, 128)
-
-        def send(d, _):
-            b_copy(g, d).start()
-            return 0
-
-        lax.fori_loop(1, 16, send, 0)
+        for d in range(1, 4):
+            b_arrival(g, d).wait_recv()
+        total = s2[g, u].astype(F32)
+        for d in range(1, 4):
+            total = total + r2[g, (u + d) % 4].astype(F32)
+        s4[g] = total.astype(BF16)
+        for d in range(1, 4):
+            y_copy(g, d).start()
 
     def owner_send(g):
-        def wait(d, _):
-            b_arrival(g, d).wait_recv()
-            return 0
-
-        lax.fori_loop(1, 16, wait, 0)
-        r2[g, chip] = s2[g, chip]
-        total = r2[g, 0].astype(F32)
-        for i in range(1, 16):
-            total = total + r2[g, i].astype(F32)
-        s3[g] = total * jnp.where(core == 0, SCALE, 1.0)
+        for d in range(1, 4):
+            y_arrival(g, d).wait_recv()
+        total = s4[g, v].astype(F32)
+        for d in range(1, 4):
+            total = total + r4[g, (v + d) % 4].astype(F32)
+        total = total * jnp.where(core == 0, SCALE, 1.0)
+        for chunk in range(4):
+            for half in range(2):
+                at = chunk * 24 + half * 8
+                s3[g, chunk, half] = total[at : at + 16].astype(BF16)
         for chunk in range(4):
             for half in range(2):
                 if chunk == 0:
@@ -309,7 +374,7 @@
 
                     @pl.when(mine)
                     def _(half=half):
-                        r3[g, core, cx] = s3[g, half * 8 : half * 8 + 16, :]
+                        r3[g, core, u] = s3[g, 0, half]
 
                     @pl.when(jnp.logical_not(mine))
                     def _(half=half):
@@ -317,9 +382,30 @@
                 else:
                     o_copy(g, chunk, half).start()
 
+    def below_arrived(g):
+        for c in range(NC - 1):
+            here = (ctx > c) & (ctx != 2) if c == 0 else ctx > c
+
+            @pl.when(here)
+            def _(c=c):
+                for kind in range(2):
+                    k_arrival(g, kind, c).wait_recv()
+
+    def send_below(g):
+        @pl.when(ctx == 3)
+        def _():
+            for kind in range(2):
+                p_inward(g, kind).start()
+
+        for c in range(NC - 1):
+            here = (ctx == 1) if c == 0 else ctx > c
+
+            @pl.when(here)
+            def _(c=c):
+                for kind in range(2):
+                    p_copy(g, kind, c).start()
+
     def group(g, _):
-        each_below(lambda kind, c: k_arrival(g, kind, c).wait_recv())
-        c_arrival(g).wait_recv()
         q = qs[g]
         do = dos[g]
         qt = q.T
@@ -327,7 +413,11 @@
         high = jnp.full((1, QROWS), LOW, F32)
         norm = jnp.zeros((1, QROWS), F32)
         delta = jnp.zeros((1, QROWS), F32)
-        for j in range(NPB + NRB):
+        for j in ORDER_A:
+            if j == NPB:
+                below_arrived(g)
+            if j == 1:
+                c_arrival(g).wait_recv()
             keys = slice(j * BLK, (j + 1) * BLK)
             s = matmul(key_block(g, 0, j), qt)
             w = matmul(key_block(g, 1, j), dot)
@@ -350,13 +440,18 @@
         @pl.when(g < NG - 1)
         def _():
             forward_x(g + 1)
+            onward(g + 1)
 
         @pl.when(g >= 1)
         def _():
-            plane_send(g - 1)
+            swap_send(g - 1)
+
+        @pl.when(g >= 2)
+        def _():
+            owner_send(g - 2)
 
         dq = jnp.zeros((128, QROWS), F32)
-        for j in range(NPB + NRB):
+        for j in ORDER_C:
             keys = slice(j * BLK, (j + 1) * BLK)
             weight = jnp.exp2((m_s[j, 0:1, :] - high) * CEXP) * inverse
             p = e_s[keys, :] * weight
@@ -364,16 +459,16 @@
             dv = matmul(p.astype(BF16), do)
             dk = matmul(ds, q)
             if j < NPB:
-                d_prompt[0, keys, :] = dk
-                d_prompt[1, keys, :] = dv
+                s1[0, g, j] = dk.astype(BF16)
+                s1[1, g, j] = dv.astype(BF16)
+                a_copy(g, j).start()
             else:
                 b = 2 * (j - NPB)
                 sp[0, g, b : b + 2] = (dk * SCALE).astype(BF16).reshape(2, ROWS, 128)
                 sp[1, g, b : b + 2] = dv.astype(BF16).reshape(2, ROWS, 128)
+                if j == NPB + NRB - 1:
+                    send_below(g)
             dq = dq + matmul_t(key_block(g, 0, j), ds)
-        s1[g] = d_prompt[1 - core].astype(BF16)
-        a_copy(g).start()
-        each_below(lambda kind, c: p_copy(g, kind, c).start())
         dq = dq.T * SCALE
         for i in range(4):
             dq_s[pl.ds(g * 4 + i, ROWS, stride=16), :] = dq[i * ROWS : (i + 1) * ROWS, :]
@@ -384,26 +479,25 @@
 
         @pl.when(g >= 1)
         def _():
-            owner_send(g - 1)
+            inward(g - 1)
+            plane_send(g - 1)
 
         return 0
 
     lax.fori_loop(0, NG, group, 0)
-    plane_send(NG - 1)
-    dq_out[...] = dq_s[...].astype(BF16)
+    q_raw[...] = dq_s[...].astype(BF16)
+    store = pltpu.make_async_copy(q_raw, dq_out, in_sem.at[0])
+    store.start()
+    swap_send(NG - 1)
+    owner_send(NG - 2)
+    inward(NG - 1)
 
     def resp_wait(g, _):
         each_above(lambda kind, c: p_arrival(g, kind, c).wait_recv())
         return 0
 
     lax.fori_loop(0, NG, resp_wait, 0)
-    for c in range(1, NC):
-        @pl.when(ctx >= c)
-        def _(c=c):
-            for kind in range(2):
-                for g in range(NG):
-                    rp[kind, g, c] = jnp.zeros((ROWS, 128), BF16)
-
+    plane_send(NG - 1)
     for kind in range(2):
         for g in range(NG):
             total = sp[kind, g, ctx].astype(F32)
@@ -429,7 +523,9 @@
     lax.fori_loop(0, NG, owner_wait, 0)
     for kind in range(2):
         for g in range(NG):
-            total = (r3[g, kind, 0] + r3[g, kind, 1]) + (r3[g, kind, 2] + r3[g, kind, 3])
+            total = r3[g, kind, 0].astype(F32)
+            for su in range(1, 4):
+                total = total + r3[g, kind, su].astype(F32)
             fin_p[pl.ds(g, 12, stride=NG), :] = jnp.where(core == 0, total[0:12], total[4:16])
         out = dpk_out if kind == 0 else dpv_out
         out[...] = fin_p[...].astype(BF16)
@@ -438,16 +534,24 @@
         for d in range(1, NC):
             z_copy(g, d).wait_send()
             x_copy(g, d).wait_send()
+            b_copy(g, d).wait_send()
+            y_copy(g, d).wait_send()
         c_copy(g).wait_send()
-        a_copy(g).wait_send()
+        for j in range(NPB):
+            a_copy(g, j).wait_send()
         each_above(lambda kind, c: k_copy(g, kind, c).wait_send())
         each_below(lambda kind, c: p_copy(g, kind, c).wait_send())
 
-        def sent_plane(d, _):
-            b_copy(g, d).wait_send()
-            return 0
-
-        lax.fori_loop(1, 16, sent_plane, 0)
+        @pl.when(ctx == 2)
+        def _():
+            for kind in range(2):
+                k_onward(g, kind).wait_send()
+
+        @pl.when(ctx == 3)
+        def _():
+            for kind in range(2):
+                p_inward(g, kind).wait_send()
+
         for chunk in range(4):
             for half in range(2):
                 if chunk == 0:
@@ -459,6 +563,18 @@
         return 0
 
     lax.fori_loop(0, NG, sent, 0)
+    store.wait()
+
+
+def hand_over(*refs):
+    sems = refs[-1]
+    copies = [
+        pltpu.make_async_copy(refs[i], refs[5 + i], sems.at[i]) for i in range(5)
+    ]
+    for copy in copies:
+        copy.start()
+    for copy in copies:
+        copy.wait()
 
 
 def on_device(queries, grad_out, resp_keys, resp_values, prompt_keys, prompt_values, resp_lengths):
@@ -474,7 +590,7 @@
             jax.ShapeDtypeStruct((12 * NG, 128), BF16),
         ],
         in_specs=[pl.BlockSpec(memory_space=pl.ANY)] * 6 + [pl.BlockSpec(memory_space=pltpu.SMEM)],
-        out_specs=[pl.BlockSpec(memory_space=pltpu.VMEM)] * 5,
+        out_specs=[pl.BlockSpec(memory_space=pl.ANY)] + [pl.BlockSpec(memory_space=pltpu.VMEM)] * 4,
         scratch_shapes=[
             vmem((ROWS * 16, 128), BF16),
             vmem((ROWS * 16, 128), BF16),
@@ -490,15 +606,15 @@
             vmem(((NPB + NRB) * BLK, QROWS), F32),
             vmem(((NPB + NRB) * BLK, QROWS), F32),
             vmem((NPB + NRB, 8, QROWS), F32),
-            vmem((2, NPB * BLK, 128), F32),
-            vmem((8, 128), F32),
             vmem((ROWS * 16, 128), F32),
-            vmem((NG, NPB * BLK, 128), BF16),
-            vmem((NG, NPB * BLK, 128), BF16),
-            vmem((NG, 16, PIECE, 128), BF16),
-            vmem((NG, 16, PIECE, 128), BF16),
-            vmem((NG, PIECE, 128), F32),
-            vmem((NG, 2, 4, 16, 128), F32),
+            vmem((2, NG, NPB, BLK, 128), BF16),
+            vmem((NG, NPB, BLK, 128), BF16),
+            vmem((NG, 4, 4, PIECE, 128), BF16),
+            vmem((NG, 4, 4, PIECE, 128), BF16),
+            vmem((NG, 4, PIECE, 128), BF16),
+            vmem((NG, 4, PIECE, 128), BF16),
+            vmem((NG, 4, 2, 16, 128), BF16),
+            vmem((NG, 2, 4, 16, 128), BF16),
             vmem((2, NG, NC, ROWS, 128), BF16),
             vmem((2, NG, NC, ROWS, 128), BF16),
             vmem((ROWS * NG, 128), F32),
@@ -508,8 +624,9 @@
             dma((NG, 3)), dma((NG, 3)),
             dma((NG,)), dma((NG,)),
             dma((NG, 2, NC)), dma((NG, 2, NC)),
-            dma((NG,)), dma((NG,)),
-            dma((NG, 16)), dma((NG, 16)),
+            dma((NG, NPB)), dma((NG, NPB)),
+            dma((NG, 3)), dma((NG, 3)),
+            dma((NG, 3)), dma((NG, 3)),
             dma((NG, 4, 2)), dma((NG, 2, 4)),
             dma((NG, 2, NC)), dma((NG, 2, NC)),
         ],
@@ -526,6 +643,16 @@
         prompt_values.reshape(PROWS * NG, 128),
         resp_lengths,
     )
+    anywhere = pl.BlockSpec(memory_space=pl.ANY)
+    outs = pl.pallas_call(
+        hand_over,
+        out_shape=[jax.ShapeDtypeStruct(x.shape, x.dtype) for x in outs],
+        in_specs=[anywhere] * 5,
+        out_specs=[anywhere] * 5,
+        scratch_shapes=[dma((5,))],
+        compiler_params=pltpu.CompilerParams(vmem_limit_bytes=56 * 1024 * 1024),
+        name="hand_over",
+    )(*outs)
     return (
         outs[0].reshape(queries.shape),
         outs[1].reshape(resp_keys.shape),

time: 102 us -> 120 us (1.18); the launches traced: 101 us -> 120 us
  Pallas kernels: 94.4 us -> 119 us
  local copies, waits for them, and re-layouts: 5.2 us -> 0 us
    pallas_call x0 -> x1, Pallas kernels: none -> 37.6 us  [on_device(): pl.pallas_call(hand_over, out_shape=[jax.ShapeDtypeStruct(x.shape, x.dtyp...]
    pallas_call x1, Pallas kernels: 94.4 us -> 81.3 us  [on_device(): pl.pallas_call(kernel, out_shape=[jax.ShapeDtypeStruct((ROWS * 16, 128),...]
    unnamed x13 -> x0, local copies, waits for them, and re-layouts: 5.2 us -> none
where the time goes in v2:
time: 120 us
  Pallas kernels  119 us (99%)
  between operations  1.29 us (1%)
    pallas_call x1, Pallas kernels, on_device(): pl.pallas_call(kernel, out_shape=[jax.ShapeDtypeStruct((ROWS * 16, 128),...  81.3 us
    pallas_call x1, Pallas kernels, on_device(): pl.pallas_call(hand_over, out_shape=[jax.ShapeDtypeStruct(x.shape, x.dtyp...  37.6 us

profile of v2, /device:TPU:1, one launch (start us, length us, event | category | flops | bytes accessed | tf_op | source)
XLA Modules:
  0.0 120.3 jit_solution(14671633150928254888)
XLA Ops:
  1.3 81.3 %attention_backward.1 = (bf16[3072,128]{1,0:T(8,128)(2,1)}, bf16[768,128]{1,0:T(8,128)(2,1)}, bf16[768,128]{1,0:T(8,128)(2,1)}, bf16[48,128]{1,0:T(8,128)(2,1)}, bf16[48,128]{1,0:T(8,128)(2,1)}) custom-call(bf16[3072,128]{1,0:T(8,128)(2,1)} %bitcast.11, bf16[3072,128]{1,0:T(8,128)(2,1)} %bitcast.12, bf16[768,128]{1,0:T(8,128)(2,1)} %bitcast.15, ...), custom_call_target="tpu_custom_call" | custom-call | tf_op jit(solution)/shard_map/attention_backward/pallas_call | solution.py:583
  82.6 37.6 %hand_over.1 = (bf16[3072,128]{1,0:T(8,128)(2,1)}, bf16[768,128]{1,0:T(8,128)(2,1)}, bf16[768,128]{1,0:T(8,128)(2,1)}, bf16[48,128]{1,0:T(8,128)(2,1)}, bf16[48,128]{1,0:T(8,128)(2,1)}) custom-call(bf16[3072,128]{1,0:T(8,128)(2,1)} %get-tuple-element.15.refs_0_, bf16[768,128]{1,0:T(8,128)(2,1)} %get-tuple-element.16.refs_1_, ...), custom_call_target="tpu_custom_call" | custom-call | tf_op jit(solution)/shard_map/hand_over/pallas_call | solution.py:647

commit v3 on v2

--- a/solution.py
+++ b/solution.py
@@ -24,7 +24,7 @@
 PIECE = 96
 LOW = -1e30
 ORDER_A = (0, 4, 5, 1, 2, 3)
-ORDER_C = (4, 5, 0, 1, 2, 3)
+ORDER_C = (0, 1, 2, 3, 4, 5)
 
 
 def matmul(a, b):
@@ -40,9 +40,9 @@
     dq_out, drk_out, drv_out, dpk_out, dpv_out,
     q_raw, do_raw, rk_raw, rv_raw, pk_raw, pv_raw,
     tmp, pkv, rkv, qs, dos, e_s, w_s, m_s, dq_s,
-    s1, r1, s2, r2, s4, r4, s3, r3, sp, rp, fin_r, fin_p,
+    s1, r1, s2, r2, s4, r4, s3, r3, sp, rp, fin_r, fin_p, fin_b,
     in_sem,
-    z_send, z_recv, x_send, x_recv, c_send, c_recv, k_send, k_recv,
+    z_send, z_recv, w_send, w_recv, x_send, x_recv, c_send, c_recv, k_send, k_recv,
     a_send, a_recv, b_send, b_recv, y_send, y_recv, o_send, o_recv, p_send, p_recv,
 ):
     ctx = lax.axis_index("ctx")
@@ -117,15 +117,13 @@
     for b in range(1, NC):
         @pl.when(ctx < b)
         def _(b=b):
-            for kind in range(2):
-                for g in range(NG):
-                    rkv[kind, g, b] = jnp.zeros((ROWS, 128), BF16)
+            for g in range(NG):
+                rkv[g, b] = jnp.zeros((2, ROWS, 128), BF16)
 
         @pl.when((ctx >= b) | ((ctx == 0) & (b == NC - 1)))
         def _(b=b):
-            for kind in range(2):
-                for g in range(NG):
-                    rp[kind, g, b] = jnp.zeros((ROWS, 128), BF16)
+            for g in range(NG):
+                rp[g, b] = jnp.zeros((2, ROWS, 128), BF16)
 
     for kind in range(2):
         loads[kind].wait()
@@ -138,7 +136,7 @@
         raw = rk_raw if kind == 0 else rv_raw
         tmp[0 : ROWS * NG, :] = raw[...].astype(F32)
         for g in range(NG):
-            rkv[kind, g, ctx] = tmp[pl.ds(g, ROWS, stride=NG), :].astype(BF16)
+            rkv[g, ctx, kind] = tmp[pl.ds(g, ROWS, stride=NG), :].astype(BF16)
 
     @pl.when(is_self)
     def _():
@@ -173,6 +171,18 @@
             x_send.at[g, d - 1], x_recv.at[g, d - 1], {"resp": v_at(4 - d)},
         )
 
+    def w_copy(d):
+        return remote(
+            pkv.at[core, u, pl.ds(1, 3), v], pkv.at[core, u, pl.ds(1, 3), v],
+            w_send.at[d - 1], w_recv.at[u], {"resp": u_at(d)},
+        )
+
+    def w_arrival(g):
+        return remote(
+            pkv.at[core, g, pl.ds(1, 3), v], pkv.at[core, g, pl.ds(1, 3), v],
+            w_send.at[0], w_recv.at[g], {"resp": plane_at(g, v)},
+        )
+
     def c_copy(g):
         return remote(
             pkv.at[core, g, pl.ds(1, 3)], pkv.at[core, g, pl.ds(1, 3)],
@@ -185,22 +195,19 @@
             c_send.at[g], c_recv.at[g], {"resp": other},
         )
 
-    def k_copy(g, kind, to):
-        return remote(
-            rkv.at[kind, g, ctx], rkv.at[kind, g, ctx],
-            k_send.at[g, kind, to], k_recv.at[g, kind, ctx], {"ctx": to},
-        )
-
-    def k_arrival(g, kind, src):
-        return remote(
-            rkv.at[kind, g, src], rkv.at[kind, g, src],
-            k_send.at[g, kind, src], k_recv.at[g, kind, src], {"ctx": src},
-        )
-
-    def k_onward(g, kind):
-        return remote(
-            rkv.at[kind, g, 0], rkv.at[kind, g, 0],
-            k_send.at[g, kind, 0], k_recv.at[g, kind, 0], {"ctx": 3},
+    def k_copy(g, to):
+        return remote(
+            rkv.at[g, ctx], rkv.at[g, ctx], k_send.at[g, to], k_recv.at[g, ctx], {"ctx": to}
+        )
+
+    def k_arrival(g, src):
+        return remote(
+            rkv.at[g, src], rkv.at[g, src], k_send.at[g, src], k_recv.at[g, src], {"ctx": src}
+        )
+
+    def k_onward(g):
+        return remote(
+            rkv.at[g, 0], rkv.at[g, 0], k_send.at[g, 0], k_recv.at[g, 0], {"ctx": 3}
         )
 
     def a_copy(g, j):
@@ -208,17 +215,16 @@
             s1.at[1 - core, g, j], r1.at[g, j], a_send.at[g, j], a_recv.at[g, j], {"resp": other}
         )
 
-    def b_copy(g, d):
-        return remote(
-            s2.at[g, (u + d) % 4], r2.at[g, u],
-            b_send.at[g, d - 1], b_recv.at[g, d - 1], {"resp": u_at(d)},
-        )
-
-    def b_arrival(g, d):
-        src = (u + 4 - d) % 4
+    def b_copy(g, to):
+        return remote(
+            s2.at[g, to], r2.at[g, u],
+            b_send.at[g, to], b_recv.at[g, u], {"resp": plane_at(to, v)},
+        )
+
+    def b_arrival(g, src):
         return remote(
             s2.at[g, src], r2.at[g, src],
-            b_send.at[g, d - 1], b_recv.at[g, d - 1], {"resp": u_at(4 - d)},
+            b_send.at[g, src], b_recv.at[g, src], {"resp": plane_at(src, v)},
         )
 
     def y_copy(g, d):
@@ -246,65 +252,86 @@
             o_send.at[g, su, kind], o_recv.at[g, kind, su], source(su, kind),
         )
 
-    def p_copy(g, kind, to):
-        return remote(
-            sp.at[kind, g, to], rp.at[kind, g, ctx],
-            p_send.at[g, kind, to], p_recv.at[g, kind, ctx], {"ctx": to},
-        )
-
-    def p_arrival(g, kind, src):
-        return remote(
-            sp.at[kind, g, src], rp.at[kind, g, src],
-            p_send.at[g, kind, src], p_recv.at[g, kind, src], {"ctx": src},
-        )
-
-    def p_inward(g, kind):
-        return remote(
-            sp.at[kind, g, 0], rp.at[kind, g, 0],
-            p_send.at[g, kind, 0], p_recv.at[g, kind, 0], {"ctx": 2},
+    def p_copy(g, to):
+        return remote(
+            sp.at[g, to], rp.at[g, ctx], p_send.at[g, to], p_recv.at[g, ctx], {"ctx": to}
+        )
+
+    def p_arrival(g, src):
+        return remote(
+            sp.at[g, src], rp.at[g, src], p_send.at[g, src], p_recv.at[g, src], {"ctx": src}
+        )
+
+    def p_inward(g):
+        return remote(
+            sp.at[g, 0], rp.at[g, 0], p_send.at[g, 0], p_recv.at[g, 0], {"ctx": 2}
         )
 
     def each_above(body):
         for c in range(1, NC):
             @pl.when((ctx < c) & ((ctx > 0) | (c < NC - 1)))
             def _(c=c):
-                for kind in range(2):
-                    body(kind, c)
+                body(c)
 
     def each_below(body):
         for c in range(NC - 1):
             @pl.when((ctx > c) & ((ctx < NC - 1) | (c > 0)))
             def _(c=c):
-                for kind in range(2):
-                    body(kind, c)
-
-    def send_first(g, _):
+                body(c)
+
+    def send_resp(g):
+        for c in (2, 3, 1):
+            here = (ctx < c) & (ctx > 0) if c == 3 else ctx < c
+
+            @pl.when(here)
+            def _(c=c):
+                k_copy(g, c).start()
+
+    for d in range(1, NC):
+        z_copy(0, d).start()
+    send_resp(0)
+
+    def import_rest():
         for d in range(1, NC):
-            z_copy(g, d).start()
-        each_above(lambda kind, c: k_copy(g, kind, c).start())
-        return 0
-
-    lax.fori_loop(0, NG, send_first, 0)
+            z_copy(1, d).start()
+
+        @pl.when(u > 1)
+        def _():
+            for d in range(1, NC):
+                z_copy(u, d).start()
+
+    def spread_u():
+        @pl.when(u > 1)
+        def _():
+            for d in range(1, NC):
+                z_arrival(u, d).wait_recv()
+            for d in range(1, NC):
+                w_copy(d).start()
 
     def onward(g):
         @pl.when(ctx == 2)
         def _():
-            for kind in range(2):
-                k_arrival(g, kind, 0).wait_recv()
-                k_onward(g, kind).start()
+            k_arrival(g, 0).wait_recv()
+            k_onward(g).start()
 
     def inward(g):
         @pl.when(ctx == 2)
         def _():
-            for kind in range(2):
-                p_inward(g, kind).wait_recv()
-                total = sp[kind, g, 0].astype(F32) + rp[kind, g, 0].astype(F32)
-                sp[kind, g, 0] = total.astype(BF16)
-                p_copy(g, kind, 0).start()
+            p_inward(g).wait_recv()
+            total = sp[g, 0].astype(F32) + rp[g, 0].astype(F32)
+            sp[g, 0] = total.astype(BF16)
+            p_copy(g, 0).start()
 
     def forward_x(g):
-        for d in range(1, NC):
-            z_arrival(g, d).wait_recv()
+        @pl.when(g <= 1)
+        def _():
+            for d in range(1, NC):
+                z_arrival(g, d).wait_recv()
+
+        @pl.when((g > 1) & (u != g))
+        def _():
+            w_arrival(g).wait_recv()
+
         for d in range(1, NC):
             x_copy(g, d).start()
 
@@ -329,26 +356,29 @@
     forward_x(0)
     position = first + lax.broadcasted_iota(jnp.int32, (ROWS, 128), 0)
     take_heads(loads[5], do_raw, dos, position < length)
+    onward(0)
     forward_core(0)
-    onward(0)
+    import_rest()
+    send_resp(1)
 
     def key_block(g, kind, j):
         if j < NPB:
             return pkv[kind, g, j].reshape(BLK, 128)
         b = j - NPB
-        return rkv[kind, g, 2 * b : 2 * b + 2].reshape(BLK, 128)
-
-    def swap_send(g):
-        for j in range(NPB):
-            a_copy(g, j).wait_recv()
-            total = s1[core, g, j].astype(F32) + r1[g, j].astype(F32)
-            s2[g, j] = total.astype(BF16).reshape(4, PIECE, 128)
-        for d in range(1, 4):
-            b_copy(g, d).start()
+        return rkv[g, 2 * b : 2 * b + 2, kind].reshape(BLK, 128)
+
+    def swap_block(g, j):
+        a_copy(g, j).wait_recv()
+        total = s1[core, g, j].astype(F32) + r1[g, j].astype(F32)
+        s2[g, j] = total.astype(BF16).reshape(4, PIECE, 128)
+
+        @pl.when(u != j)
+        def _():
+            b_copy(g, j).start()
 
     def plane_send(g):
         for d in range(1, 4):
-            b_arrival(g, d).wait_recv()
+            b_arrival(g, (u + d) % 4).wait_recv()
         total = s2[g, u].astype(F32)
         for d in range(1, 4):
             total = total + r2[g, (u + d) % 4].astype(F32)
@@ -388,22 +418,62 @@
 
             @pl.when(here)
             def _(c=c):
-                for kind in range(2):
-                    k_arrival(g, kind, c).wait_recv()
+                k_arrival(g, c).wait_recv()
 
     def send_below(g):
         @pl.when(ctx == 3)
         def _():
-            for kind in range(2):
-                p_inward(g, kind).start()
+            p_inward(g).start()
 
         for c in range(NC - 1):
             here = (ctx == 1) if c == 0 else ctx > c
 
             @pl.when(here)
             def _(c=c):
-                for kind in range(2):
-                    p_copy(g, kind, c).start()
+                p_copy(g, c).start()
+
+    def resp_finish(g):
+        each_above(lambda c: p_arrival(g, c).wait_recv())
+        for kind in range(2):
+            total = sp[g, ctx, kind].astype(F32)
+            for c in range(1, NC):
+                total = total + rp[g, c, kind].astype(F32)
+            fin_r[kind, pl.ds(g, ROWS, stride=NG), :] = total
+
+    def middle(g):
+        @pl.when(g < NG - 1)
+        def _():
+            forward_x(g + 1)
+            onward(g + 1)
+
+        @pl.when(g == 0)
+        def _():
+            spread_u()
+
+        @pl.when(g >= 1)
+        def _():
+            inward(g - 1)
+
+        @pl.when(g >= 2)
+        def _():
+            owner_send(g - 2)
+
+    def ending(g):
+        send_below(g)
+        swap_block(g, 3)
+
+        @pl.when(g < NG - 1)
+        def _():
+            forward_core(g + 1)
+
+        @pl.when(g < NG - 2)
+        def _():
+            send_resp(g + 2)
+
+        @pl.when(g >= 1)
+        def _():
+            plane_send(g - 1)
+            resp_finish(g - 1)
 
     def group(g, _):
         q = qs[g]
@@ -437,19 +507,7 @@
         inverse = 1.0 / norm
         delta = delta * inverse
 
-        @pl.when(g < NG - 1)
-        def _():
-            forward_x(g + 1)
-            onward(g + 1)
-
-        @pl.when(g >= 1)
-        def _():
-            swap_send(g - 1)
-
-        @pl.when(g >= 2)
-        def _():
-            owner_send(g - 2)
-
+        middle(g)
         dq = jnp.zeros((128, QROWS), F32)
         for j in ORDER_C:
             keys = slice(j * BLK, (j + 1) * BLK)
@@ -464,50 +522,34 @@
                 a_copy(g, j).start()
             else:
                 b = 2 * (j - NPB)
-                sp[0, g, b : b + 2] = (dk * SCALE).astype(BF16).reshape(2, ROWS, 128)
-                sp[1, g, b : b + 2] = dv.astype(BF16).reshape(2, ROWS, 128)
-                if j == NPB + NRB - 1:
-                    send_below(g)
+                sp[g, b : b + 2, 0] = (dk * SCALE).astype(BF16).reshape(2, ROWS, 128)
+                sp[g, b : b + 2, 1] = dv.astype(BF16).reshape(2, ROWS, 128)
+                if j == NPB:
+                    for i in range(3):
+                        swap_block(g, i)
             dq = dq + matmul_t(key_block(g, 0, j), ds)
         dq = dq.T * SCALE
         for i in range(4):
             dq_s[pl.ds(g * 4 + i, ROWS, stride=16), :] = dq[i * ROWS : (i + 1) * ROWS, :]
 
-        @pl.when(g < NG - 1)
-        def _():
-            forward_core(g + 1)
-
-        @pl.when(g >= 1)
-        def _():
-            inward(g - 1)
-            plane_send(g - 1)
-
+        ending(g)
         return 0
 
     lax.fori_loop(0, NG, group, 0)
     q_raw[...] = dq_s[...].astype(BF16)
     store = pltpu.make_async_copy(q_raw, dq_out, in_sem.at[0])
     store.start()
-    swap_send(NG - 1)
     owner_send(NG - 2)
     inward(NG - 1)
-
-    def resp_wait(g, _):
-        each_above(lambda kind, c: p_arrival(g, kind, c).wait_recv())
-        return 0
-
-    lax.fori_loop(0, NG, resp_wait, 0)
     plane_send(NG - 1)
+    owner_send(NG - 1)
+    resp_finish(NG - 1)
+    stores = [store]
     for kind in range(2):
-        for g in range(NG):
-            total = sp[kind, g, ctx].astype(F32)
-            for c in range(1, NC):
-                total = total + rp[kind, g, c].astype(F32)
-            fin_r[pl.ds(g, ROWS, stride=NG), :] = total
-        out = drk_out if kind == 0 else drv_out
-        out[...] = fin_r[...].astype(BF16)
-
-    owner_send(NG - 1)
+        held = rk_raw if kind == 0 else rv_raw
+        held[...] = fin_r[kind].astype(BF16)
+        stores.append(pltpu.make_async_copy(held, drk_out if kind == 0 else drv_out, in_sem.at[1 + kind]))
+        stores[-1].start()
 
     def owner_wait(g, _):
         for sx in range(4):
@@ -527,30 +569,28 @@
             for su in range(1, 4):
                 total = total + r3[g, kind, su].astype(F32)
             fin_p[pl.ds(g, 12, stride=NG), :] = jnp.where(core == 0, total[0:12], total[4:16])
-        out = dpk_out if kind == 0 else dpv_out
-        out[...] = fin_p[...].astype(BF16)
+        fin_b[kind] = fin_p[...].astype(BF16)
+        stores.append(pltpu.make_async_copy(fin_b.at[kind], dpk_out if kind == 0 else dpv_out, in_sem.at[3 + kind]))
+        stores[-1].start()
 
     def sent(g, _):
         for d in range(1, NC):
-            z_copy(g, d).wait_send()
             x_copy(g, d).wait_send()
-            b_copy(g, d).wait_send()
+            b_copy(g, (u + d) % 4).wait_send()
             y_copy(g, d).wait_send()
         c_copy(g).wait_send()
         for j in range(NPB):
             a_copy(g, j).wait_send()
-        each_above(lambda kind, c: k_copy(g, kind, c).wait_send())
-        each_below(lambda kind, c: p_copy(g, kind, c).wait_send())
+        each_above(lambda c: k_copy(g, c).wait_send())
+        each_below(lambda c: p_copy(g, c).wait_send())
 
         @pl.when(ctx == 2)
         def _():
-            for kind in range(2):
-                k_onward(g, kind).wait_send()
+            k_onward(g).wait_send()
 
         @pl.when(ctx == 3)
         def _():
-            for kind in range(2):
-                p_inward(g, kind).wait_send()
+            p_inward(g).wait_send()
 
         for chunk in range(4):
             for half in range(2):
@@ -563,17 +603,30 @@
         return 0
 
     lax.fori_loop(0, NG, sent, 0)
-    store.wait()
+    for d in range(1, NC):
+        z_copy(0, d).wait_send()
+        z_copy(1, d).wait_send()
+
+    @pl.when(u > 1)
+    def _():
+        for d in range(1, NC):
+            z_copy(u, d).wait_send()
+            w_copy(d).wait_send()
+
+    for copy in stores:
+        copy.wait()
 
 
 def hand_over(*refs):
     sems = refs[-1]
-    copies = [
-        pltpu.make_async_copy(refs[i], refs[5 + i], sems.at[i]) for i in range(5)
-    ]
-    for copy in copies:
+    into = [pltpu.make_async_copy(refs[i], refs[10 + i], sems.at[0, i]) for i in range(5)]
+    out = [pltpu.make_async_copy(refs[10 + i], refs[5 + i], sems.at[1, i]) for i in range(5)]
+    for copy in into:
         copy.start()
-    for copy in copies:
+    for i in range(5):
+        into[i].wait()
+        out[i].start()
+    for copy in out:
         copy.wait()
 
 
@@ -590,7 +643,7 @@
             jax.ShapeDtypeStruct((12 * NG, 128), BF16),
         ],
         in_specs=[pl.BlockSpec(memory_space=pl.ANY)] * 6 + [pl.BlockSpec(memory_space=pltpu.SMEM)],
-        out_specs=[pl.BlockSpec(memory_space=pl.ANY)] + [pl.BlockSpec(memory_space=pltpu.VMEM)] * 4,
+        out_specs=[pl.BlockSpec(memory_space=pl.ANY)] * 5,
         scratch_shapes=[
             vmem((ROWS * 16, 128), BF16),
             vmem((ROWS * 16, 128), BF16),
@@ -600,7 +653,7 @@
             vmem((PROWS * NG, 128), BF16),
             vmem((ROWS * 16, 128), F32),
             vmem((2, NG, 4, 4, PIECE, 128), BF16),
-            vmem((2, NG, NC, ROWS, 128), BF16),
+            vmem((NG, NC, 2, ROWS, 128), BF16),
             vmem((NG, QROWS, 128), BF16),
             vmem((NG, QROWS, 128), BF16),
             vmem(((NPB + NRB) * BLK, QROWS), F32),
@@ -615,20 +668,22 @@
             vmem((NG, 4, PIECE, 128), BF16),
             vmem((NG, 4, 2, 16, 128), BF16),
             vmem((NG, 2, 4, 16, 128), BF16),
-            vmem((2, NG, NC, ROWS, 128), BF16),
-            vmem((2, NG, NC, ROWS, 128), BF16),
-            vmem((ROWS * NG, 128), F32),
+            vmem((NG, NC, 2, ROWS, 128), BF16),
+            vmem((NG, NC, 2, ROWS, 128), BF16),
+            vmem((2, ROWS * NG, 128), F32),
             vmem((12 * NG, 128), F32),
+            vmem((2, 12 * NG, 128), BF16),
             dma((6,)),
             dma((NG, 3)), dma((NG, 3)),
+            dma((3,)), dma((NG,)),
             dma((NG, 3)), dma((NG, 3)),
             dma((NG,)), dma((NG,)),
-            dma((NG, 2, NC)), dma((NG, 2, NC)),
+            dma((NG, NC)), dma((NG, NC)),
             dma((NG, NPB)), dma((NG, NPB)),
-            dma((NG, 3)), dma((NG, 3)),
+            dma((NG, 4)), dma((NG, 4)),
             dma((NG, 3)), dma((NG, 3)),
             dma((NG, 4, 2)), dma((NG, 2, 4)),
-            dma((NG, 2, NC)), dma((NG, 2, NC)),
+            dma((NG, NC)), dma((NG, NC)),
         ],
         compiler_params=pltpu.CompilerParams(
             collective_id=0, has_side_effects=True, vmem_limit_bytes=56 * 1024 * 1024,
@@ -649,7 +704,7 @@
         out_shape=[jax.ShapeDtypeStruct(x.shape, x.dtype) for x in outs],
         in_specs=[anywhere] * 5,
         out_specs=[anywhere] * 5,
-        scratch_shapes=[dma((5,))],
+        scratch_shapes=[pltpu.VMEM(x.shape, x.dtype) for x in outs] + [dma((2, 5))],
         compiler_params=pltpu.CompilerParams(vmem_limit_bytes=56 * 1024 * 1024),
         name="hand_over",
     )(*outs)

time: 120 us -> 76.8 us (0.64)
  Pallas kernels: 119 us -> 75.3 us
    pallas_call x1, Pallas kernels: 37.6 us -> 2.23 us  [on_device(): pl.pallas_call(hand_over, out_shape=[jax.ShapeDtypeStruct(x.shape, x.dtyp...]
    pallas_call x1, Pallas kernels: 81.3 us -> 73.1 us  [on_device(): pl.pallas_call(kernel, out_shape=[jax.ShapeDtypeStruct((ROWS * 16, 128),...]
where the time goes in v3:
time: 76.8 us; the launch traced here: 76.6 us
  Pallas kernels  75.3 us (98%)
  between operations  1.29 us (2%)
    pallas_call x1, Pallas kernels, on_device(): pl.pallas_call(kernel, out_shape=[jax.ShapeDtypeStruct((ROWS * 16, 128),...  73.1 us
    pallas_call x1, Pallas kernels, on_device(): pl.pallas_call(hand_over, out_shape=[jax.ShapeDtypeStruct(x.shape, x.dtyp...  2.23 us

profile of v3, /device:TPU:1, one launch (start us, length us, event | category | flops | bytes accessed | tf_op | source)
XLA Modules:
  0.0 76.6 jit_solution(2622258261307893752)
XLA Ops:
  1.3 73.1 %attention_backward.1 = (bf16[3072,128]{1,0:T(8,128)(2,1)}, bf16[768,128]{1,0:T(8,128)(2,1)}, bf16[768,128]{1,0:T(8,128)(2,1)}, bf16[48,128]{1,0:T(8,128)(2,1)}, bf16[48,128]{1,0:T(8,128)(2,1)}) custom-call(bf16[3072,128]{1,0:T(8,128)(2,1)} %bitcast.11, bf16[3072,128]{1,0:T(8,128)(2,1)} %bitcast.12, bf16[768,128]{1,0:T(8,128)(2,1)} %bitcast.15, ...), custom_call_target="tpu_custom_call" | custom-call | tf_op jit(solution)/shard_map/attention_backward/pallas_call | solution.py:636
  74.4 2.2 %hand_over.1 = (bf16[3072,128]{1,0:T(8,128)(2,1)}, bf16[768,128]{1,0:T(8,128)(2,1)}, bf16[768,128]{1,0:T(8,128)(2,1)}, bf16[48,128]{1,0:T(8,128)(2,1)}, bf16[48,128]{1,0:T(8,128)(2,1)}) custom-call(bf16[3072,128]{1,0:T(8,128)(2,1)} %get-tuple-element.15.refs_0_, bf16[768,128]{1,0:T(8,128)(2,1)} %get-tuple-element.16.refs_1_, ...), custom_call_target="tpu_custom_call" | custom-call | tf_op jit(solution)/shard_map/hand_over/pallas_call | solution.py:702

commit v4 on v3

v4 whole, which is shorter than its diff:
```python
import functools

import jax
import jax.numpy as jnp
from jax import lax
from jax.experimental import pallas as pl
from jax.experimental.pallas import tpu as pltpu
from jax.sharding import PartitionSpec as P

F32 = jnp.float32
BF16 = jnp.bfloat16
MESH = pl.DeviceIdType.MESH
SCALE = 128 ** -0.5
LOG2E = 1.4426950408889634
CEXP = SCALE * LOG2E
NG = 4
NC = 4
ROWS = 192
PROWS = 384
QROWS = 768
BLK = 384
NPB = 4
NRB = 2
PIECE = 96
LOW = -1e30
ORDER_A = (0, 1, 2, 3, 4, 5)
ORDER_C = (4, 5, 0, 1, 2, 3)


def matmul(a, b):
    return lax.dot_general(a, b, (((1,), (0,)), ((), ())), preferred_element_type=F32)


def matmul_t(a, b):
    return lax.dot_general(a, b, (((0,), (0,)), ((), ())), preferred_element_type=F32)


def kernel(
    q_hbm, do_hbm, rk_hbm, rv_hbm, pk_hbm, pv_hbm, len_ref,
    dq_out, drk_out, drv_out, dpk_out, dpv_out,
    q_raw, do_raw, rk_raw, rv_raw, pk_raw, pv_raw,
    tmp, pkv, rkv, qs, dos, e_s, w_s, m_s, ds_s, dq_s,
    s1, r1, s2, r2, s4, r4, s3, r3, sp, rp, fin_r, fin_p, fin_b,
    in_sem,
    z_send, z_recv, w_send, w_recv, x_send, x_recv, c_send, c_recv, k_send, k_recv,
    a_send, a_recv, b_send, b_recv, y_send, y_recv, o_send, o_recv, p_send, p_recv,
):
    ctx = lax.axis_index("ctx")
    resp = lax.axis_index("resp")
    core = resp % 2
    chip = resp // 2
    cx = chip // 4
    cy = chip % 4
    other = resp + 1 - 2 * core
    u = jnp.where(core == 0, cx, cy)
    v = jnp.where(core == 0, cy, cx)
    is_self = (u == 0) & (v == cx) & (cy == 0)

    def remote(src, dst, send, recv, to):
        return pltpu.make_async_remote_copy(
            src_ref=src, dst_ref=dst, send_sem=send, recv_sem=recv,
            device_id=to, device_id_type=MESH,
        )

    def ctx_at(d):
        return (ctx + d) % NC

    def plane_at(pu, pv):
        return (pu * (4 - 3 * core) + pv * (1 + 3 * core)) * 2 + core

    def u_at(d):
        return plane_at((u + d) % 4, v)

    def v_at(d):
        return plane_at(u, (v + d) % 4)

    def owner(chunk, half):
        return {"ctx": (ctx + u) % NC, "resp": (v * 4 + chunk) * 2 + half}

    def source(su, kind):
        at = su * (4 - 3 * kind) + cx * (1 + 3 * kind)
        return {"ctx": (ctx + NC - su) % NC, "resp": at * 2 + kind}

    barrier = pltpu.get_barrier_semaphore()

    def greet(to):
        pl.semaphore_signal(barrier, inc=1, device_id=to, device_id_type=MESH)

    loads = []
    for i, (src, dst) in enumerate(
        ((pk_hbm, pk_raw), (pv_hbm, pv_raw), (rk_hbm, rk_raw), (rv_hbm, rv_raw), (q_hbm, q_raw), (do_hbm, do_raw))
    ):
        load = pltpu.make_async_copy(src, dst, in_sem.at[i])
        load.start()
        loads.append(load)

    for d in range(1, NC):
        greet({"ctx": ctx_at(d)})

    for d in range(1, 4):
        greet({"resp": u_at(d)})
        greet({"resp": v_at(d)})
    greet({"resp": other})
    for a in range(4):
        for h in range(2):
            own_to = is_self & (core == h) if a == 0 else False

            def greet_pair(a=a, h=h):
                greet(owner(a, h))
                greet(source(a, h))

            if a == 0:
                pl.when(jnp.logical_not(own_to))(greet_pair)
            else:
                greet_pair()

    for b in range(1, NC):
        @pl.when(ctx < b)
        def _(b=b):
            for g in range(NG):
                rkv[g, b] = jnp.zeros((2, ROWS, 128), BF16)

        @pl.when((ctx >= b) | ((ctx == 0) & (b == NC - 1)))
        def _(b=b):
            for g in range(NG):
                rp[g, b] = jnp.zeros((2, ROWS, 128), BF16)

    for kind in range(2):
        loads[kind].wait()
        raw = pk_raw if kind == 0 else pv_raw
        tmp[0 : PROWS * NG, :] = raw[...].astype(F32)
        for g in range(NG):
            pkv[kind, g, 0] = tmp[pl.ds(g, PROWS, stride=NG), :].astype(BF16).reshape(4, PIECE, 128)
    for kind in range(2):
        loads[2 + kind].wait()
        raw = rk_raw if kind == 0 else rv_raw
        tmp[0 : ROWS * NG, :] = raw[...].astype(F32)
        for g in range(NG):
            rkv[g, ctx, kind] = tmp[pl.ds(g, ROWS, stride=NG), :].astype(BF16)

    @pl.when(is_self)
    def _():
        pl.semaphore_wait(barrier, 24)

    @pl.when(jnp.logical_not(is_self))
    def _():
        pl.semaphore_wait(barrier, 26)

    def z_copy(g, d):
        return remote(
            pkv.at[core, g, 0, v], pkv.at[core, g, NC - d, v],
            z_send, z_recv.at[g], {"ctx": ctx_at(d)},
        )

    def arrived(ref, sem):
        remote(ref, ref, z_send, sem, {"resp": other}).wait_recv()

    def left(ref, sem):
        remote(ref, ref, sem, z_recv.at[0], {"resp": other}).wait_send()

    def x_copy(g, d):
        part = pkv.at[core, g, pl.ds(1, 3), v]
        return remote(part, part, x_send, x_recv.at[g], {"resp": v_at(d)})

    def w_copy(d):
        part = pkv.at[core, u, pl.ds(1, 3), v]
        return remote(part, part, w_send, w_recv.at[u], {"resp": u_at(d)})

    def c_copy(g):
        part = pkv.at[core, g, pl.ds(1, 3)]
        return remote(part, part, c_send, c_recv.at[g], {"resp": other})

    def k_copy(g, to):
        return remote(
            rkv.at[g, ctx], rkv.at[g, ctx],
            k_send, k_recv.at[g, jnp.minimum(ctx, 1)], {"ctx": to},
        )

    def k_onward(g):
        return remote(rkv.at[g, 0], rkv.at[g, 0], k_send, k_recv.at[g, 0], {"ctx": 3})

    def a_copy(g, j):
        return remote(
            s1.at[1 - core, g, j], r1.at[g, j], a_send, a_recv.at[g, j // 3], {"resp": other}
        )

    def b_copy(g, to):
        return remote(
            s2.at[g, to], r2.at[g, u], b_send, b_recv.at[g], {"resp": plane_at(to, v)}
        )

    def y_copy(g, d):
        return remote(s4.at[g, (v + d) % 4], r4.at[g, v], y_send, y_recv.at[g], {"resp": v_at(d)})

    def o_copy(g, chunk, half):
        return remote(
            s3.at[g * 8 + chunk * 2 + half], r3.at[g * 8 + core * 4 + u],
            o_send, o_recv, owner(chunk, half),
        )

    def p_copy(g, to):
        return remote(
            sp.at[g, to], rp.at[g, ctx], p_send, p_recv.at[g, 1], {"ctx": to}
        )

    def p_inward(g):
        return remote(sp.at[g, 0], rp.at[g, 0], p_send, p_recv.at[g, 0], {"ctx": 2})

    def send_resp(g):
        for c in (2, 3, 1):
            here = (ctx < c) & (ctx > 0) if c == 3 else ctx < c

            @pl.when(here)
            def _(c=c):
                k_copy(g, c).start()

    for d in range(1, NC):
        z_copy(0, d).start()

    @pl.when(u > 0)
    def _():
        for d in range(1, NC):
            z_copy(u, d).start()

    def spread_u():
        @pl.when(u > 0)
        def _():
            arrived(pkv.at[core, u, pl.ds(1, 3), v], z_recv.at[u])
            for d in range(1, NC):
                w_copy(d).start()

    def onward(g):
        @pl.when(ctx == 2)
        def _():
            arrived(rkv.at[g, 0], k_recv.at[g, 0])
            k_onward(g).start()

    def inward(g):
        @pl.when(ctx == 2)
        def _():
            arrived(rp.at[g, 0], p_recv.at[g, 0])
            total = sp[g, 0].astype(F32) + rp[g, 0].astype(F32)
            sp[g, 0] = total.astype(BF16)
            p_copy(g, 0).start()

    def forward_x(g):
        if g == 0:
            arrived(pkv.at[core, g, pl.ds(1, 3), v], z_recv.at[g])
        else:
            @pl.when(u != g)
            def _():
                arrived(pkv.at[core, g, pl.ds(1, 3), v], w_recv.at[g])

        for d in range(1, NC):
            x_copy(g, d).start()

    def forward_core(g):
        arrived(pkv.at[core, g, pl.ds(1, 3), pl.ds(0, 3)], x_recv.at[g])
        c_copy(g).start()

    length = len_ref[0]
    first = ctx * ROWS

    def take_heads(load, raw, dst, keep):
        load.wait()
        tmp[...] = raw[...].astype(F32)
        for h in range(16):
            rows = tmp[pl.ds(h, ROWS, stride=16), :]
            if keep is not None:
                rows = jnp.where(keep, rows, 0.0)
            dst[h // 4, (h % 4) * ROWS : (h % 4 + 1) * ROWS, :] = rows.astype(BF16)

    take_heads(loads[4], q_raw, qs, None)
    send_resp(0)
    forward_x(0)
    spread_u()
    position = first + lax.broadcasted_iota(jnp.int32, (ROWS, 128), 0)
    take_heads(loads[5], do_raw, dos, position < length)
    forward_core(0)
    onward(0)
    send_resp(1)
    forward_x(1)

    def key_block(g, kind, j):
        if j < NPB:
            return pkv[kind, g, j].reshape(BLK, 128)
        b = j - NPB
        return rkv[g, 2 * b : 2 * b + 2, kind].reshape(BLK, 128)

    def swap_blocks(g, blocks):
        first_block, last_block = blocks[0], blocks[-1]
        arrived(r1.at[g, pl.ds(first_block, len(blocks))], a_recv.at[g, last_block // 3])
        for j in blocks:
            total = s1[core, g, j].astype(F32) + r1[g, j].astype(F32)
            s2[g, j] = total.astype(BF16).reshape(4, PIECE, 128)

            @pl.when(u != j)
            def _(j=j):
                b_copy(g, j).start()

    def plane_send(g):
        arrived(r2.at[g, pl.ds(0, 3)], b_recv.at[g])
        total = s2[g, u].astype(F32)
        for d in range(1, 4):
            total = total + r2[g, (u + d) % 4].astype(F32)
        s4[g] = total.astype(BF16)
        for d in range(1, 4):
            y_copy(g, d).start()

    def owner_send(g):
        arrived(r4.at[g, pl.ds(0, 3)], y_recv.at[g])
        total = s4[g, v].astype(F32)
        for d in range(1, 4):
            total = total + r4[g, (v + d) % 4].astype(F32)
        total = total * jnp.where(core == 0, SCALE, 1.0)
        for chunk in range(4):
            for half in range(2):
                at = chunk * 24 + half * 8
                s3[g * 8 + chunk * 2 + half] = total[at : at + 16].astype(BF16)
        for chunk in range(4):
            for half in range(2):
                if chunk == 0:
                    mine = is_self & (core == half)

                    @pl.when(mine)
                    def _(half=half):
                        r3[g * 8 + core * 4 + u] = s3[g * 8 + half]

                    @pl.when(jnp.logical_not(mine))
                    def _(half=half):
                        o_copy(g, 0, half).start()
                else:
                    o_copy(g, chunk, half).start()

    def below_arrived(g):
        @pl.when((ctx == 1) | (ctx == 3))
        def _():
            arrived(rkv.at[g, 0], k_recv.at[g, 0])

        @pl.when(ctx == 2)
        def _():
            arrived(rkv.at[g, 1], k_recv.at[g, 1])

        @pl.when(ctx == 3)
        def _():
            arrived(rkv.at[g, pl.ds(1, 2)], k_recv.at[g, 1])

    def send_below(g):
        @pl.when(ctx == 3)
        def _():
            p_inward(g).start()

        for c in range(NC - 1):
            here = (ctx == 1) if c == 0 else ctx > c

            @pl.when(here)
            def _(c=c):
                p_copy(g, c).start()

    def resp_finish(g):
        @pl.when(ctx < 2)
        def _():
            arrived(rp.at[g, pl.ds(0, 2)], p_recv.at[g, 1])

        @pl.when(ctx == 2)
        def _():
            arrived(rp.at[g, 3], p_recv.at[g, 1])

        for kind in range(2):
            total = sp[g, ctx, kind].astype(F32)
            for c in range(1, NC):
                total = total + rp[g, c, kind].astype(F32)
            fin_r[kind, pl.ds(g, ROWS, stride=NG), :] = total

    def middle(g):
        @pl.when(g == 0)
        def _():
            forward_x(2)

        @pl.when(g >= 1)
        def _():
            inward(g - 1)

        @pl.when(g >= 2)
        def _():
            owner_send(g - 2)

    def later(g):
        send_below(g)

        @pl.when(g < NG - 1)
        def _():
            forward_core(g + 1)
            onward(g + 1)

        @pl.when(g < NG - 2)
        def _():
            send_resp(g + 2)

        @pl.when(g >= 1)
        def _():
            plane_send(g - 1)

    def ending(g):
        @pl.when(g == 0)
        def _():
            forward_x(3)

        swap_blocks(g, (3,))

        @pl.when(g >= 1)
        def _():
            resp_finish(g - 1)

    def group(g, _):
        q = qs[g]
        do = dos[g]
        qt = q.T
        dot = do.T
        high = jnp.full((1, QROWS), LOW, F32)
        norm = jnp.zeros((1, QROWS), F32)
        delta = jnp.zeros((1, QROWS), F32)
        for j in ORDER_A:
            if j == NPB:
                below_arrived(g)
            if j == 1:
                arrived(pkv.at[1 - core, g, pl.ds(1, 3)], c_recv.at[g])
            keys = slice(j * BLK, (j + 1) * BLK)
            s = matmul(key_block(g, 0, j), qt)
            w = matmul(key_block(g, 1, j), dot)
            w_s[keys, :] = w
            if j >= NPB:
                r = lax.broadcasted_iota(jnp.int32, (BLK, QROWS), 0) + (j - NPB) * BLK
                t = lax.broadcasted_iota(jnp.int32, (1, QROWS), 1) % ROWS + first
                s = jnp.where(r <= t, s, LOW)
            new = jnp.maximum(high, jnp.max(s, axis=0, keepdims=True))
            e = jnp.exp2((s - new) * CEXP)
            e_s[keys, :] = e
            m_s[j, 0:1, :] = new
            fix = jnp.exp2((high - new) * CEXP)
            norm = norm * fix + jnp.sum(e, axis=0, keepdims=True)
            delta = delta * fix + jnp.sum(e * w, axis=0, keepdims=True)
            high = new
        inverse = 1.0 / norm
        delta = delta * inverse

        middle(g)
        for j in ORDER_C:
            keys = slice(j * BLK, (j + 1) * BLK)
            weight = jnp.exp2((m_s[j, 0:1, :] - high) * CEXP) * inverse
            p = e_s[keys, :] * weight
            ds = (p * (w_s[keys, :] - delta)).astype(BF16)
            dv = matmul(p.astype(BF16), do)
            dk = matmul(ds, q)
            if j < NPB:
                s1[0, g, j] = dk.astype(BF16)
                s1[1, g, j] = dv.astype(BF16)
                a_copy(g, j).start()
                if j == NPB - 1:
                    swap_blocks(g, (0, 1, 2))
            else:
                b = 2 * (j - NPB)
                sp[g, b : b + 2, 0] = (dk * SCALE).astype(BF16).reshape(2, ROWS, 128)
                sp[g, b : b + 2, 1] = dv.astype(BF16).reshape(2, ROWS, 128)
                if j == NPB + NRB - 1:
                    later(g)
            ds_s[g, keys, :] = ds
        ending(g)
        return 0

    lax.fori_loop(0, NG, group, 0)
    def query_part(g):
        dq = jnp.zeros((128, QROWS), F32)
        for j in range(NPB + NRB):
            dq = dq + matmul_t(key_block(g, 0, j), ds_s[g, j * BLK : (j + 1) * BLK, :])
        dq = dq.T * SCALE
        for i in range(4):
            dq_s[pl.ds(g * 4 + i, ROWS, stride=16), :] = dq[i * ROWS : (i + 1) * ROWS, :]

    query_part(0)
    owner_send(NG - 2)
    inward(NG - 1)
    query_part(1)
    query_part(2)
    plane_send(NG - 1)
    query_part(3)
    q_raw[...] = dq_s[...].astype(BF16)
    store = pltpu.make_async_copy(q_raw, dq_out, in_sem.at[0])
    store.start()
    owner_send(NG - 1)
    resp_finish(NG - 1)
    stores = [store]
    for kind in range(2):
        held = rk_raw if kind == 0 else rv_raw
        held[...] = fin_r[kind].astype(BF16)
        stores.append(pltpu.make_async_copy(held, drk_out if kind == 0 else drv_out, in_sem.at[1 + kind]))
        stores[-1].start()

    @pl.when(u == 0)
    def _():
        left(pkv.at[core, 0, pl.ds(0, 3), 0], z_send)

    @pl.when(u > 0)
    def _():
        left(pkv.at[core, 0, pl.ds(0, 3), pl.ds(0, 2)], z_send)
        left(pkv.at[core, 0, pl.ds(1, 3), pl.ds(0, 3)], w_send)

    left(pkv.at[core, :, pl.ds(1, 3), pl.ds(0, 3)], x_send)
    left(pkv.at[core, :, pl.ds(1, 3)], c_send)

    @pl.when(ctx < 3)
    def _():
        left(rkv.at[:, pl.ds(0, 2)], k_send)

    left(s1.at[0], a_send)
    left(s2.at[:, pl.ds(0, 3)], b_send)
    left(s4.at[:, pl.ds(0, 3)], y_send)
    for c in range(1, NC):
        @pl.when(ctx == c)
        def _(c=c):
            left(sp.at[:, pl.ds(0, c)], p_send)

    @pl.when(is_self)
    def _():
        left(s3.at[pl.ds(0, 28)], o_send)
        arrived(r3.at[pl.ds(0, 28)], o_recv)

    @pl.when(jnp.logical_not(is_self))
    def _():
        left(s3, o_send)
        arrived(r3, o_recv)

    for kind in range(2):
        for g in range(NG):
            total = r3[g * 8 + kind * 4].astype(F32)
            for su in range(1, 4):
                total = total + r3[g * 8 + kind * 4 + su].astype(F32)
            fin_p[pl.ds(g, 12, stride=NG), :] = jnp.where(core == 0, total[0:12], total[4:16])
        fin_b[kind] = fin_p[...].astype(BF16)
        stores.append(pltpu.make_async_copy(fin_b.at[kind], dpk_out if kind == 0 else dpv_out, in_sem.at[3 + kind]))
        stores[-1].start()

    for copy in stores:
        copy.wait()


def hand_over(*refs):
    sems = refs[-1]
    into = [pltpu.make_async_copy(refs[i], refs[10 + i], sems.at[0, i]) for i in range(5)]
    out = [pltpu.make_async_copy(refs[10 + i], refs[5 + i], sems.at[1, i]) for i in range(5)]
    for copy in into:
        copy.start()
    for i in range(5):
        into[i].wait()
        out[i].start()
    for copy in out:
        copy.wait()


def on_device(queries, grad_out, resp_keys, resp_values, prompt_keys, prompt_values, resp_lengths):
    dma = pltpu.SemaphoreType.DMA
    vmem = pltpu.VMEM
    outs = pl.pallas_call(
        kernel,
        out_shape=[
            jax.ShapeDtypeStruct((ROWS * 16, 128), BF16),
            jax.ShapeDtypeStruct((ROWS * NG, 128), BF16),
            jax.ShapeDtypeStruct((ROWS * NG, 128), BF16),
            jax.ShapeDtypeStruct((12 * NG, 128), BF16),
            jax.ShapeDtypeStruct((12 * NG, 128), BF16),
        ],
        in_specs=[pl.BlockSpec(memory_space=pl.ANY)] * 6 + [pl.BlockSpec(memory_space=pltpu.SMEM)],
        out_specs=[pl.BlockSpec(memory_space=pl.ANY)] * 5,
        scratch_shapes=[
            vmem((ROWS * 16, 128), BF16),
            vmem((ROWS * 16, 128), BF16),
            vmem((ROWS * NG, 128), BF16),
            vmem((ROWS * NG, 128), BF16),
            vmem((PROWS * NG, 128), BF16),
            vmem((PROWS * NG, 128), BF16),
            vmem((ROWS * 16, 128), F32),
            vmem((2, NG, 4, 4, PIECE, 128), BF16),
            vmem((NG, NC, 2, ROWS, 128), BF16),
            vmem((NG, QROWS, 128), BF16),
            vmem((NG, QROWS, 128), BF16),
            vmem(((NPB + NRB) * BLK, QROWS), F32),
            vmem(((NPB + NRB) * BLK, QROWS), F32),
            vmem((NPB + NRB, 8, QROWS), F32),
            vmem((NG, (NPB + NRB) * BLK, QROWS), BF16),
            vmem((ROWS * 16, 128), F32),
            vmem((2, NG, NPB, BLK, 128), BF16),
            vmem((NG, NPB, BLK, 128), BF16),
            vmem((NG, 4, 4, PIECE, 128), BF16),
            vmem((NG, 4, 4, PIECE, 128), BF16),
            vmem((NG, 4, PIECE, 128), BF16),
            vmem((NG, 4, PIECE, 128), BF16),
            vmem((NG * 8, 16, 128), BF16),
            vmem((NG * 8, 16, 128), BF16),
            vmem((NG, NC, 2, ROWS, 128), BF16),
            vmem((NG, NC, 2, ROWS, 128), BF16),
            vmem((2, ROWS * NG, 128), F32),
            vmem((12 * NG, 128), F32),
            vmem((2, 12 * NG, 128), BF16),
            dma((6,)),
            dma, dma((NG,)),
            dma, dma((NG,)),
            dma, dma((NG,)),
            dma, dma((NG,)),
            dma, dma((NG, 2)),
            dma, dma((NG, 2)),
            dma, dma((NG,)),
            dma, dma((NG,)),
            dma, dma,
            dma, dma((NG, 2)),
        ],
        compiler_params=pltpu.CompilerParams(
            collective_id=0, has_side_effects=True, vmem_limit_bytes=56 * 1024 * 1024,
        ),
        name="attention_backward",
    )(
        queries.reshape(ROWS * 16, 128),
        grad_out.reshape(ROWS * 16, 128),
        resp_keys.reshape(ROWS * NG, 128),
        resp_values.reshape(ROWS * NG, 128),
        prompt_keys.reshape(PROWS * NG, 128),
        prompt_values.reshape(PROWS * NG, 128),
        resp_lengths,
    )
    anywhere = pl.BlockSpec(memory_space=pl.ANY)
    outs = pl.pallas_call(
        hand_over,
        out_shape=[jax.ShapeDtypeStruct(x.shape, x.dtype) for x in outs],
        in_specs=[anywhere] * 5,
        out_specs=[anywhere] * 5,
        scratch_shapes=[pltpu.VMEM(x.shape, x.dtype) for x in outs] + [dma((2, 5))],
        compiler_params=pltpu.CompilerParams(vmem_limit_bytes=56 * 1024 * 1024),
        name="hand_over",
    )(*outs)
    return (
        outs[0].reshape(queries.shape),
        outs[1].reshape(resp_keys.shape),
        outs[2].reshape(resp_values.shape),
        outs[3].reshape(12, NG, 128),
        outs[4].reshape(12, NG, 128),
    )


def solution(mesh):
    heads = P("resp", "ctx", "head", None)
    prompt = P("ctx", "head", None)
    owners = P(("ctx", "resp"), "head", None)
    return jax.shard_map(
        on_device,
        mesh=mesh,
        in_specs=(heads, heads, heads, heads, prompt, prompt, P("resp")),
        out_specs=(heads, heads, heads, owners, owners),
        check_vma=False,
    )
```

time: 76.8 us -> 72.9 us (0.949)
  Pallas kernels: 75.3 us -> 70.8 us
    pallas_call x1, Pallas kernels: 73.1 us -> 68.6 us  [on_device(): pl.pallas_call(kernel, out_shape=[jax.ShapeDtypeStruct((ROWS * 16, 128),...]
where the time goes in v4:
time: 72.9 us; the launch traced here: 72.3 us
  Pallas kernels  70.8 us (97%)
  between operations  1.45 us (2%)
    pallas_call x1, Pallas kernels, on_device(): pl.pallas_call(kernel, out_shape=[jax.ShapeDtypeStruct((ROWS * 16, 128),...  68.6 us
    pallas_call x1, Pallas kernels, on_device(): pl.pallas_call(hand_over, out_shape=[jax.ShapeDtypeStruct(x.shape, x.dtyp...  2.23 us

profile of v4, /device:TPU:1, one launch (start us, length us, event | category | flops | bytes accessed | tf_op | source)
XLA Modules:
  0.0 72.3 jit_solution(4707566107258238524)
XLA Ops:
  1.3 68.6 %attention_backward.1 = (bf16[3072,128]{1,0:T(8,128)(2,1)}, bf16[768,128]{1,0:T(8,128)(2,1)}, bf16[768,128]{1,0:T(8,128)(2,1)}, bf16[48,128]{1,0:T(8,128)(2,1)}, bf16[48,128]{1,0:T(8,128)(2,1)}) custom-call(bf16[3072,128]{1,0:T(8,128)(2,1)} %bitcast.11, bf16[3072,128]{1,0:T(8,128)(2,1)} %bitcast.12, bf16[768,128]{1,0:T(8,128)(2,1)} %bitcast.15, ...), custom_call_target="tpu_custom_call" | custom-call | tf_op jit(solution)/shard_map/attention_backward/pallas_call | solution.py:563
  69.9 2.2 %hand_over.1 = (bf16[3072,128]{1,0:T(8,128)(2,1)}, bf16[768,128]{1,0:T(8,128)(2,1)}, bf16[768,128]{1,0:T(8,128)(2,1)}, bf16[48,128]{1,0:T(8,128)(2,1)}, bf16[48,128]{1,0:T(8,128)(2,1)}) custom-call(bf16[3072,128]{1,0:T(8,128)(2,1)} %get-tuple-element.15.refs_0_, bf16[768,128]{1,0:T(8,128)(2,1)} %get-tuple-element.16.refs_1_, ...), custom_call_target="tpu_custom_call" | custom-call | tf_op jit(solution)/shard_map/hand_over/pallas_call | solution.py:630

commit v5 on v4

--- a/solution.py
+++ b/solution.py
@@ -54,7 +54,7 @@
     other = resp + 1 - 2 * core
     u = jnp.where(core == 0, cx, cy)
     v = jnp.where(core == 0, cy, cx)
-    is_self = (u == 0) & (v == cx) & (cy == 0)
+    is_self = cy == 0
 
     def remote(src, dst, send, recv, to):
         return pltpu.make_async_remote_copy(
@@ -75,11 +75,10 @@
         return plane_at(u, (v + d) % 4)
 
     def owner(chunk, half):
-        return {"ctx": (ctx + u) % NC, "resp": (v * 4 + chunk) * 2 + half}
-
-    def source(su, kind):
-        at = su * (4 - 3 * kind) + cx * (1 + 3 * kind)
-        return {"ctx": (ctx + NC - su) % NC, "resp": at * 2 + kind}
+        return {"ctx": (ctx + cy) % NC, "resp": (cx * 4 + chunk) * 2 + half}
+
+    def source(sy, kind):
+        return {"ctx": (ctx + NC - sy) % NC, "resp": (cx * 4 + sy) * 2 + kind}
 
     barrier = pltpu.get_barrier_semaphore()
 
@@ -194,7 +193,7 @@
 
     def o_copy(g, chunk, half):
         return remote(
-            s3.at[g * 8 + chunk * 2 + half], r3.at[g * 8 + core * 4 + u],
+            s3.at[g * 8 + chunk * 2 + half], r3.at[g * 8 + core * 4 + cy],
             o_send, o_recv, owner(chunk, half),
         )
 
@@ -292,11 +291,12 @@
         arrived(r1.at[g, pl.ds(first_block, len(blocks))], a_recv.at[g, last_block // 3])
         for j in blocks:
             total = s1[core, g, j].astype(F32) + r1[g, j].astype(F32)
-            s2[g, j] = total.astype(BF16).reshape(4, PIECE, 128)
-
-            @pl.when(u != j)
-            def _(j=j):
-                b_copy(g, j).start()
+            for x in range(4):
+                part = total[x * PIECE : (x + 1) * PIECE].astype(BF16)
+                s2[g, jnp.where(core == 0, x, j), jnp.where(core == 0, j, x)] = part
+        if last_block == NPB - 1:
+            for d in range(1, 4):
+                b_copy(g, (u + d) % 4).start()
 
     def plane_send(g):
         arrived(r2.at[g, pl.ds(0, 3)], b_recv.at[g])
@@ -324,7 +324,7 @@
 
                     @pl.when(mine)
                     def _(half=half):
-                        r3[g * 8 + core * 4 + u] = s3[g * 8 + half]
+                        r3[g * 8 + core * 4 + cy] = s3[g * 8 + half]
 
                     @pl.when(jnp.logical_not(mine))
                     def _(half=half):
@@ -381,10 +381,6 @@
         def _():
             inward(g - 1)
 
-        @pl.when(g >= 2)
-        def _():
-            owner_send(g - 2)
-
     def later(g):
         send_below(g)
 
@@ -397,7 +393,7 @@
         def _():
             send_resp(g + 2)
 
-        @pl.when(g >= 1)
+        @pl.when(g == NG - 1)
         def _():
             plane_send(g - 1)
 
@@ -408,9 +404,14 @@
 
         swap_blocks(g, (3,))
 
-        @pl.when(g >= 1)
-        def _():
-            resp_finish(g - 1)
+        @pl.when((g >= 1) & (g < NG - 1))
+        def _():
+            plane_send(g - 1)
+
+        @pl.when(g >= 2)
+        def _():
+            owner_send(g - 2)
+            resp_finish(g - 2)
 
     def group(g, _):
         q = qs[g]
@@ -487,6 +488,7 @@
     q_raw[...] = dq_s[...].astype(BF16)
     store = pltpu.make_async_copy(q_raw, dq_out, in_sem.at[0])
     store.start()
+    resp_finish(NG - 2)
     owner_send(NG - 1)
     resp_finish(NG - 1)
     stores = [store]

time: 72.9 us -> 69.9 us (0.959)
  Pallas kernels: 70.8 us -> 68.3 us
    pallas_call x1, Pallas kernels: 68.6 us -> 66.1 us  [on_device(): pl.pallas_call(kernel, out_shape=[jax.ShapeDtypeStruct((ROWS * 16, 128),...]
where the time goes in v5:
time: 69.9 us; the launch traced here: 69.8 us
  Pallas kernels  68.3 us (98%)
  between operations  1.45 us (2%)
    pallas_call x1, Pallas kernels, on_device(): pl.pallas_call(kernel, out_shape=[jax.ShapeDtypeStruct((ROWS * 16, 128),...  66.1 us
    pallas_call x1, Pallas kernels, on_device(): pl.pallas_call(hand_over, out_shape=[jax.ShapeDtypeStruct(x.shape, x.dtyp...  2.23 us

profile of v5, /device:TPU:1, one launch (start us, length us, event | category | flops | bytes accessed | tf_op | source)
XLA Modules:
  0.0 69.8 jit_solution(1499471225316528842)
XLA Ops:
  1.3 66.1 %attention_backward.1 = (bf16[3072,128]{1,0:T(8,128)(2,1)}, bf16[768,128]{1,0:T(8,128)(2,1)}, bf16[768,128]{1,0:T(8,128)(2,1)}, bf16[48,128]{1,0:T(8,128)(2,1)}, bf16[48,128]{1,0:T(8,128)(2,1)}) custom-call(bf16[3072,128]{1,0:T(8,128)(2,1)} %bitcast.11, bf16[3072,128]{1,0:T(8,128)(2,1)} %bitcast.12, bf16[768,128]{1,0:T(8,128)(2,1)} %bitcast.15, ...), custom_call_target="tpu_custom_call" | custom-call | tf_op jit(solution)/shard_map/attention_backward/pallas_call | solution.py:565
  67.4 2.2 %hand_over.1 = (bf16[3072,128]{1,0:T(8,128)(2,1)}, bf16[768,128]{1,0:T(8,128)(2,1)}, bf16[768,128]{1,0:T(8,128)(2,1)}, bf16[48,128]{1,0:T(8,128)(2,1)}, bf16[48,128]{1,0:T(8,128)(2,1)}) custom-call(bf16[3072,128]{1,0:T(8,128)(2,1)} %get-tuple-element.15.refs_0_, bf16[768,128]{1,0:T(8,128)(2,1)} %get-tuple-element.16.refs_1_, ...), custom_call_target="tpu_custom_call" | custom-call | tf_op jit(solution)/shard_map/hand_over/pallas_call | solution.py:632

commit v6 on v5

--- a/solution.py
+++ b/solution.py
@@ -271,10 +271,10 @@
 
     take_heads(loads[4], q_raw, qs, None)
     send_resp(0)
+    position = first + lax.broadcasted_iota(jnp.int32, (ROWS, 128), 0)
+    take_heads(loads[5], do_raw, dos, position < length)
     forward_x(0)
     spread_u()
-    position = first + lax.broadcasted_iota(jnp.int32, (ROWS, 128), 0)
-    take_heads(loads[5], do_raw, dos, position < length)
     forward_core(0)
     onward(0)
     send_resp(1)
@@ -402,7 +402,9 @@
         def _():
             forward_x(3)
 
-        swap_blocks(g, (3,))
+        @pl.when(g == NG - 1)
+        def _():
+            swap_blocks(g, (3,))
 
         @pl.when((g >= 1) & (g < NG - 1))
         def _():
@@ -425,6 +427,11 @@
             if j == NPB:
                 below_arrived(g)
             if j == 1:
+                @pl.when(g >= 1)
+                def _():
+                    swap_blocks(g - 1, (0, 1, 2))
+                    swap_blocks(g - 1, (3,))
+
                 arrived(pkv.at[1 - core, g, pl.ds(1, 3)], c_recv.at[g])
             keys = slice(j * BLK, (j + 1) * BLK)
             s = matmul(key_block(g, 0, j), qt)
@@ -458,7 +465,9 @@
                 s1[1, g, j] = dv.astype(BF16)
                 a_copy(g, j).start()
                 if j == NPB - 1:
-                    swap_blocks(g, (0, 1, 2))
+                    @pl.when(g == NG - 1)
+                    def _():
+                        swap_blocks(g, (0, 1, 2))
             else:
                 b = 2 * (j - NPB)
                 sp[g, b : b + 2, 0] = (dk * SCALE).astype(BF16).reshape(2, ROWS, 128)

time: 69.9 us -> 69 us (0.987)
  Pallas kernels: 68.3 us -> 67.4 us
    pallas_call x1, Pallas kernels: 66.1 us -> 65.2 us  [on_device(): pl.pallas_call(kernel, out_shape=[jax.ShapeDtypeStruct((ROWS * 16, 128),...]
where the time goes in v6:
time: 69 us; the launch traced here: 68.8 us
  Pallas kernels  67.4 us (98%)
  between operations  1.45 us (2%)
    pallas_call x1, Pallas kernels, on_device(): pl.pallas_call(kernel, out_shape=[jax.ShapeDtypeStruct((ROWS * 16, 128),...  65.2 us
    pallas_call x1, Pallas kernels, on_device(): pl.pallas_call(hand_over, out_shape=[jax.ShapeDtypeStruct(x.shape, x.dtyp...  2.23 us

profile of v6, /device:TPU:1, one launch (start us, length us, event | category | flops | bytes accessed | tf_op | source)
XLA Modules:
  0.0 68.8 jit_solution(7967510364070006139)
XLA Ops:
  1.3 65.2 %attention_backward.1 = (bf16[3072,128]{1,0:T(8,128)(2,1)}, bf16[768,128]{1,0:T(8,128)(2,1)}, bf16[768,128]{1,0:T(8,128)(2,1)}, bf16[48,128]{1,0:T(8,128)(2,1)}, bf16[48,128]{1,0:T(8,128)(2,1)}) custom-call(bf16[3072,128]{1,0:T(8,128)(2,1)} %bitcast.11, bf16[3072,128]{1,0:T(8,128)(2,1)} %bitcast.12, bf16[768,128]{1,0:T(8,128)(2,1)} %bitcast.15, ...), custom_call_target="tpu_custom_call" | custom-call | tf_op jit(solution)/shard_map/attention_backward/pallas_call | solution.py:574
  66.4 2.2 %hand_over.1 = (bf16[3072,128]{1,0:T(8,128)(2,1)}, bf16[768,128]{1,0:T(8,128)(2,1)}, bf16[768,128]{1,0:T(8,128)(2,1)}, bf16[48,128]{1,0:T(8,128)(2,1)}, bf16[48,128]{1,0:T(8,128)(2,1)}) custom-call(bf16[3072,128]{1,0:T(8,128)(2,1)} %get-tuple-element.15.refs_0_, bf16[768,128]{1,0:T(8,128)(2,1)} %get-tuple-element.16.refs_1_, ...), custom_call_target="tpu_custom_call" | custom-call | tf_op jit(solution)/shard_map/hand_over/pallas_call | solution.py:641
